TPU v7x, 32 devices: a whole 2x2x4 slice. The times are simulated.
32 devices in a mesh: wide: 16 (over z, y, core), narrow: 2 (over x).
Axes of the slice: x: 2, y: 2, z: 4, core: 2. Of those that a mesh axis runs over, the one named last changes fastest.
Arguments:
- train_points: float32 [512, 3, 256], P('wide'), may hold values from 0 to 2
- train_weights: bfloat16 [512, 256, 128], P(('wide', 'narrow')), may hold values from -1 to 1
- train_counts: int32 [512], P('wide'), may hold values from 64 to 256
- test_points: float32 [64, 3, 128], P(('wide', 'narrow')), may hold values from 0 to 2
- prior: bfloat16 [64, 128, 128], P(('wide', 'narrow')), may hold values from -6 to 6
- test_counts: int32 [64], P(('wide', 'narrow')), may hold values from 32 to 128
- pair_count: int32 [512], P('wide'), may hold values from 1 to 40, as said below
- pair_slot: int32 [16, 1280], P('wide'), may hold values from 0 to 15
- slot_tile: int32 [16, 16], replicated, may hold values from 0 to 3
Outputs:
- posterior: bfloat16 [64, 128, 128], P(('wide', 'narrow'))
Inputs may be any that keep to these rules, and one draw needn't show every extreme that they name: `pair_count`: each training tile has 1 to 40 pairs; in every draw all 16 tiles of some one device have 40. `pair_slot`: positions of a group's list at or past the sum of its tiles' pair counts are not read.
All inputs are finite; a program needn't handle non-finite values.
Results may differ from a plain program's by a relative error of at most 0.0041.
Values may be sent and summed in bfloat16 or wider, within the bound.
No kernel may reach another device: no remote copies, remote signals or barrier semaphores. Data moves between devices by JAX's collectives and lax.ppermute only.
A program may use at most 64 MiB of HBM per device.

v0:
```python
import jax
import jax.numpy as jnp
from jax import lax
from jax.sharding import PartitionSpec as P

radius = 1.0
block_pairs = 16


def wendland(test_rows, train_rows):
    spread = test_rows[:, 0, :, None] - train_rows[:, 0, None, :]
    square = spread * spread
    for coord_id in (1, 2):
        spread = test_rows[:, coord_id, :, None] - train_rows[:, coord_id, None, :]
        square = square + spread * spread
    scaled = jnp.sqrt(square) / radius
    falloff = jnp.maximum(1.0 - scaled, 0.0)
    return falloff**4 * (4.0 * scaled + 1.0)


def body(
    train_points,
    train_weights,
    train_counts,
    test_points,
    prior,
    test_counts,
    pair_count,
    pair_slot,
    slot_tile,
):
    narrow_size = lax.axis_size("narrow")
    narrow_id = lax.axis_index("narrow")
    wide_id = lax.axis_index("wide")
    train_group = pair_count.shape[0]
    own_tiles = train_weights.shape[0]
    slot_count = slot_tile.shape[0]
    test_group = test_points.shape[0] * narrow_size
    list_length = pair_slot.shape[1]
    lane_ids = jnp.arange(train_weights.shape[1], dtype=jnp.int32)
    own_counts = lax.dynamic_slice_in_dim(train_counts, narrow_id * own_tiles, own_tiles)
    masked = jnp.where(
        (lane_ids[None, :] < own_counts[:, None])[:, :, None],
        train_weights,
        jnp.zeros((), jnp.bfloat16),
    )
    group_tests = lax.all_gather(test_points, "narrow", axis=0, tiled=True)
    wanted = lax.dynamic_index_in_dim(slot_tile, wide_id, 1, keepdims=False)
    picker = (wanted[:, None] == jnp.arange(test_group, dtype=jnp.int32)[None, :]).astype(
        jnp.float32
    )
    outgoing = jnp.einsum("st,tcp->scp", picker, group_tests, precision=lax.Precision.HIGHEST)
    slot_points = lax.all_to_all(outgoing, "wide", split_axis=0, concat_axis=0, tiled=True)
    cumulative = jnp.cumsum(pair_count)
    slot_row = pair_slot[0]
    tile_ids_all = jnp.arange(train_group, dtype=jnp.int32)
    first_pair = jnp.sum(jnp.where(tile_ids_all < narrow_id * own_tiles, pair_count, 0))
    stride = 1
    own_pairs = jnp.sum(lax.dynamic_slice_in_dim(pair_count, narrow_id * own_tiles, own_tiles))
    tile_base = narrow_id * own_tiles
    offsets = jnp.arange(block_pairs, dtype=jnp.int32)

    def block_step(block_id, partial_value):
        pair_index = block_id * block_pairs + offsets
        in_range = pair_index < own_pairs
        position = jnp.minimum(first_pair + pair_index * stride, list_length - 1)
        tile_ids = jnp.sum((cumulative[None, :] <= position[:, None]).astype(jnp.int32), axis=1)
        tile_ids = jnp.minimum(tile_ids, train_group - 1)
        target = slot_row[position]
        kernel = wendland(slot_points[target], train_points[tile_ids])
        kernel = jnp.where(in_range[:, None, None], kernel, 0.0).astype(jnp.bfloat16)
        weights = masked[jnp.clip(tile_ids - tile_base, 0, masked.shape[0] - 1)]
        contribution = jnp.einsum(
            "bij,bjs->bis", kernel, weights, preferred_element_type=jnp.float32
        )
        return partial_value.at[target].add(contribution)

    partial_value = jnp.zeros(
        (slot_count, slot_points.shape[2], train_weights.shape[2]), jnp.float32
    )
    block_count = (own_pairs + block_pairs - 1) // block_pairs
    partial_value = lax.fori_loop(0, block_count, block_step, partial_value)
    grouped = jnp.einsum(
        "st,sic->tic",
        picker,
        lax.all_to_all(partial_value, "wide", split_axis=0, concat_axis=0, tiled=True),
        precision=lax.Precision.HIGHEST,
    )
    owned = lax.psum_scatter(grouped, "narrow", scatter_dimension=0, tiled=True)
    test_live = jnp.arange(prior.shape[1], dtype=jnp.int32)[None, :] < test_counts[:, None]
    update = jnp.where(test_live[:, :, None], owned, 0.0)
    return (prior.astype(jnp.float32) + update).astype(jnp.bfloat16)


def solution(mesh):
    return jax.shard_map(
        body,
        mesh=mesh,
        in_specs=(
            P("wide", None, None),
            P(("wide", "narrow"), None, None),
            P("wide"),
            P(("wide", "narrow"), None, None),
            P(("wide", "narrow"), None, None),
            P(("wide", "narrow")),
            P("wide"),
            P("wide", None),
            P(),
        ),
        out_specs=P(("wide", "narrow"), None, None),
        check_vma=False,
    )
```

profile of v0, /device:TPU:0, one launch (start us, length us, event | category | flops | bytes accessed | tf_op | source)
XLA Modules:
  0.0 459.3 jit_solution(7640013793962268431)
XLA Ops:
  7.2 5.2 %all_gather.3 = f32[4,3,128]{2,1,0:T(4,128)S(1)} all-gather(f32[2,3,128]{2,1,0:T(4,128)S(1)} %copy.33), channel_id=1, replica_groups=mesh['wide'=16,'narrow'=2] {'narrow'}, dimensions={0}, use_global_device_ids=true | all-gather | bytes 9216 | tf_op jit(solution)/shard_map/all_gather | solution.py:47
  13.5 6.5 %all-to-all-start = ((f32[16,3,128]{2,1,0:T(4,128)}), f32[16,3,128]{2,1,0:T(4,128)S(1)}, u32[]{:S(2)}, u32[]{:S(2)}) async-start(f32[16,3,128]{2,1,0:T(4,128)} %copy.35), calls=%async_computation | async-start | bytes 65536 | tf_op jit(solution)/shard_map/all_to_all | solution.py:53
  26.7 143.6 %while.11 = (s32[]{:T(128)}, f32[16,128,128]{2,1,0:T(8,128)S(1)}, s32[]{:T(128)}, s32[]{:T(128)}, s32[1280]{0:T(1024)S(1)}, /*index=5*/s32[]{:T(128)}, f32[16,3,...) while((s32[]{:T(128)}, f32[16,128,128]{2,1,0:T(8,128)S(1)}, ...), condition=%wide.region_6.7_spmd.clone, body=%wide.region_3.6_spmd.clone.sunk | while | flops 143398704 | bytes 7824957 | solution.py:82
  30.9 2.8 fusion.53
  40.5 2.8 fusion.53
  50.0 2.8 fusion.53
  59.6 2.8 fusion.53
  62.4 2.6 scatter_fusion
  69.2 2.8 fusion.53
  78.7 2.8 fusion.53
  88.3 2.8 fusion.53
  91.1 2.6 scatter_fusion
  97.9 2.8 fusion.53
  107.5 2.8 fusion.53
  117.0 2.8 fusion.53
  126.6 2.8 fusion.53
  136.2 2.8 fusion.53
  139.0 2.6 scatter_fusion
  145.7 2.8 fusion.53
  148.5 2.6 scatter_fusion
  155.3 2.8 fusion.53
  164.9 2.8 fusion.53
  170.3 267.5 %all_to_all.10 = f32[16,128,128]{2,1,0:T(8,128)S(1)} all-to-all(f32[16,128,128]{2,1,0:T(8,128)S(1)} %get-tuple-element.68), channel_id=1, replica_groups=mesh['wide'=16,'narrow'=2] {'wide'}, dimensions={0} | all-to-all | bytes 2097152 | tf_op jit(solution)/shard_map/all_to_all | solution.py:86
  439.7 11.1 %reduce-scatter.2.cloned.1.call-done = f32[2,128,128]{2,1,0:T(8,128)} async-done(((f32[4,128,128]{2,1,0:T(8,128)}), f32[2,128,128]{2,1,0:T(8,128)}) %reduce-scatter.2.cloned.1.call-update) | async-done | bytes 131088 | tf_op jit(solution)/shard_map/reduce_scatter | solution.py:89
  (300 shorter events, 101.0 us)
Async XLA Ops:
  6.5 5.9 %copy-start = (s32[16,16]{1,0:T(8,128)S(1)}, s32[16,16]{1,0:T(8,128)}, u32[]{:S(2)}) copy-start(s32[16,16]{1,0:T(8,128)} %param.19) | copy-start | bytes 3076
  13.5 13.1 %all-to-all-start = ((f32[16,3,128]{2,1,0:T(4,128)}), f32[16,3,128]{2,1,0:T(4,128)S(1)}, u32[]{:S(2)}, u32[]{:S(2)}) async-start(f32[16,3,128]{2,1,0:T(4,128)} %copy.35), calls=%async_computation | async-start | bytes 65536 | tf_op jit(solution)/shard_map/all_to_all | solution.py:53
  20.0 430.8 %reduce-scatter.2.cloned.1.call-start = ((), (), s32[]{:S(2)}) async-start(), calls=%async_computation.3 | async-start | bytes 393216 | tf_op jit(solution)/shard_map/reduce_scatter | solution.py:89
  20.9 1.8 copy-start.4
  20.9 4.1 copy-start.3
  20.9 4.1 copy-start.1
  437.8 1.8 copy-start.5
  437.8 13.0 %copy-start.2 = (bf16[2,128,128]{2,1,0:T(8,128)(2,1)S(1)}, bf16[2,128,128]{2,1,0:T(8,128)(2,1)}, u32[]{:S(2)}) copy-start(bf16[2,128,128]{2,1,0:T(8,128)(2,1)} %param.15) | copy-start | bytes 196612
Sparse Core Ops, SparseCore 0:
  439.7 11.0 reduce-scatter.1
where the time goes:
time: 462 us; the launch traced here: 459 us
  blocking collectives  273 us (59%)
  other arithmetic  65.5 us (14%)
  matrix products  43.2 us (9%)
  local copies, waits for them, and re-layouts  43 us (9%)
  between operations  14.1 us (3%)
  waiting for transfers between devices  12.7 us (3%)
  starting transfers between devices  6.54 us (1%)
    all_to_all x1, blocking collectives, body(): lax.all_to_all(partial_value, 'wide', split_axis=0, concat_axis=0, tiled=...  268 us
    dot_general x15, matrix products, block_step(): jnp.einsum('bij,bjs->bis', kernel, weights, preferred_element_type=jnp.fl...  41.9 us
    scatter-add x15, other arithmetic, block_step(): return partial_value.at[target].add(contribution)  39 us
    gather x30, local copies, waits for them, and re-layouts, block_step(): kernel = wendland(slot_points[target], train_points[tile_ids])  17.7 us
    gather x15, local copies, waits for them, and re-layouts, block_step(): weights = masked[jnp.clip(tile_ids - tile_base, 0, masked.shape[0] - 1)]  11.2 us
    reduce_scatter x1, waiting for transfers between devices, body(): owned = lax.psum_scatter(grouped, 'narrow', scatter_dimension=0, tiled=True)  11.1 us
    gather x15, local copies, waits for them, and re-layouts, block_step(): target = slot_row[position]  9.81 us
    select_n x15, other arithmetic, block_step(): target = slot_row[position]  9.54 us
  transfers between devices with their start and end apart: 2, of which 2 were waited for; matrix products, arithmetic and copies ran while one was open for 1% of the time, Pallas kernels for 0%

commit v1 on v0

v1 whole, which is shorter than its diff:
```python
import functools

import jax
import jax.numpy as jnp
from jax import lax
from jax.experimental import pallas as pl
from jax.experimental.pallas import tpu as pltpu
from jax.sharding import PartitionSpec as P

f32, bf16, i32 = jnp.float32, jnp.bfloat16, jnp.int32
ROWS = 128
COLS = 512
BLOCK = 16
VMEM_LIMIT = 48 * 1024 * 1024
VMEM = pl.BlockSpec(memory_space=pltpu.VMEM)
SMEM = pl.BlockSpec(memory_space=pltpu.SMEM)


def split3(x):
    high = x.astype(bf16).astype(f32)
    rest = x - high
    mid = rest.astype(bf16).astype(f32)
    low = (rest - mid).astype(bf16).astype(f32)
    return high, mid, low


def prepare_kernel(
    narrow_id_ref, train_counts_ref, pair_count_ref, points_ref, weights_ref, pair_slot_ref,
    packed_weights_ref, packed_points_ref, packed_times_ref,
    wide_weights, raw_points,
):
    own_tiles, tile, columns = weights_ref.shape
    slots = packed_times_ref.shape[0]
    list_length = pair_slot_ref.shape[1]
    first_tile = narrow_id_ref[0] * own_tiles
    window = tile + 128
    positions = lax.broadcasted_iota(i32, (1, list_length), 1)
    named = pair_slot_ref[...]
    one_hot = (
        lax.broadcasted_iota(i32, (slots, list_length), 0) == jnp.broadcast_to(named, (slots, list_length))
    ).astype(f32)
    row8 = lax.broadcasted_iota(i32, (8, tile), 0)
    lane = lax.broadcasted_iota(i32, (8, window), 1)
    lane_slots = lax.broadcasted_iota(i32, (slots, window), 1)

    def skip(t, total):
        return total + pair_count_ref[t]

    first_pair = lax.fori_loop(0, first_tile, skip, jnp.int32(0))

    def step(t, carry):
        offset, pair = carry
        u = points_ref[first_tile + t] - 1.0
        square = jnp.sum(u * u, axis=0, keepdims=True)
        padded = jnp.concatenate([u, jnp.zeros((8 - u.shape[0], tile), f32)], axis=0)
        raw = jnp.where(
            row8 < 3, padded, jnp.where(row8 == 3, square, jnp.where(row8 == 4, 1.0, 0.0))
        )
        pair_end = pair + pair_count_ref[first_tile + t]
        inside = jnp.logical_and(positions >= pair, positions < pair_end)
        times = jnp.sum(jnp.where(inside, one_hot, 0.0), axis=1, keepdims=True)
        shift = lax.rem(offset, 128)
        base = pl.multiple_of(offset - shift, 128)
        rolled = pltpu.roll(
            jnp.concatenate([raw, jnp.zeros((8, 128), f32)], axis=1), shift, 1
        )
        spot = pl.ds(base, window)
        raw_points[:, spot] = jnp.where(lane >= shift, rolled, raw_points[:, spot])
        packed_times_ref[:, spot] = jnp.where(
            lane_slots >= shift, times, packed_times_ref[:, spot]
        )
        wide_weights[pl.ds(offset, tile), :] = weights_ref[t].astype(f32)
        return offset + train_counts_ref[first_tile + t], pair_end

    total, _ = lax.fori_loop(0, own_tiles, step, (jnp.int32(0), first_pair))
    shift = lax.rem(total, 128)
    base = pl.multiple_of(total - shift, 128)
    tail = COLS + 128
    spot = pl.ds(base, tail)
    raw_points[:, spot] = jnp.where(
        lax.broadcasted_iota(i32, (8, tail), 1) >= shift, 0.0, raw_points[:, spot]
    )
    packed_times_ref[:, spot] = jnp.where(
        lax.broadcasted_iota(i32, (slots, tail), 1) >= shift, 0.0, packed_times_ref[:, spot]
    )
    wide_weights[pl.ds(total, COLS), :] = jnp.zeros((COLS, columns), f32)

    def finish(c, carry):
        start = pl.multiple_of(c * COLS, COLS)
        high, mid, low = split3(raw_points[:, pl.ds(start, COLS)])
        packed_points_ref[:, pl.ds(start, COLS)] = jnp.concatenate(
            [high, mid, high, mid, low, high], axis=0
        ).astype(bf16)
        packed_weights_ref[pl.ds(start, COLS), :] = wide_weights[pl.ds(start, COLS), :].astype(bf16)
        return carry

    lax.fori_loop(0, (total + COLS - 1) // COLS, finish, 0)


def prepare(narrow_id, train_counts, pair_count, points, weights, pair_slot, slots):
    own_tiles, tile, columns = weights.shape
    length = own_tiles * tile + COLS + 128
    return pl.pallas_call(
        prepare_kernel,
        out_shape=(
            jax.ShapeDtypeStruct((length, columns), bf16),
            jax.ShapeDtypeStruct((48, length), bf16),
            jax.ShapeDtypeStruct((slots, length), f32),
        ),
        in_specs=[SMEM, SMEM, SMEM, VMEM, VMEM, VMEM],
        out_specs=(VMEM, VMEM, VMEM),
        scratch_shapes=[pltpu.VMEM((length, columns), f32), pltpu.VMEM((8, length), f32)],
        compiler_params=pltpu.CompilerParams(vmem_limit_bytes=VMEM_LIMIT),
        cost_estimate=pl.CostEstimate(flops=40_000_000, bytes_accessed=4_000_000, transcendentals=0),
        name="prepare",
    )(narrow_id, train_counts, pair_count, points, weights, pair_slot)


def main_kernel(
    narrow_id_ref, train_counts_ref, received_ref, packed_weights_ref, packed_points_ref, packed_times_ref,
    partial_ref,
    rows_ref, sums_ref, block_slot, slot_row,
):
    slots, test_tile, columns = partial_ref.shape
    senders = received_ref.shape[0] // slots
    own_tiles = train_counts_ref.shape[0] // senders
    first_tile = narrow_id_ref[0] * own_tiles
    total = lax.fori_loop(
        0, own_tiles, lambda t, a: a + train_counts_ref[first_tile + t], jnp.int32(0)
    )
    row8 = lax.broadcasted_iota(i32, (8, test_tile), 0)
    per_slot = test_tile // BLOCK

    def place(g, offset):
        got = received_ref[g * senders]
        for s in range(1, senders):
            got = got + received_ref[g * senders + s]
        count = jnp.max(got[3:4, :]).astype(i32)
        v = jnp.concatenate([got, got], axis=0) - 1.0
        square = jnp.sum(jnp.where(row8 < 3, v * v, 0.0), axis=0, keepdims=True)
        raw = jnp.where(
            row8 < 3, -2.0 * v, jnp.where(row8 == 3, 1.0, jnp.where(row8 == 4, square, 0.0))
        )
        high, mid, low = split3(raw)
        operand = jnp.concatenate([high, high, mid, mid, high, low], axis=0)
        rows_ref[pl.ds(pl.multiple_of(offset * BLOCK, BLOCK), test_tile), :] = operand.T.astype(bf16)
        slot_row[g] = offset
        for b in range(per_slot):
            block_slot[offset + b] = g
        return offset + (count + BLOCK - 1) // BLOCK

    blocks = lax.fori_loop(0, slots, place, jnp.int32(0))
    per_tile = ROWS // BLOCK
    for b in range(per_tile):
        block_slot[blocks + b] = 0
    row_tiles = (blocks + per_tile - 1) // per_tile
    col_tiles = (total + COLS - 1) // COLS

    def row_step(r, carry):
        row_start = pl.multiple_of(r * ROWS, ROWS)
        left = rows_ref[pl.ds(row_start, ROWS), :]

        def col_step(c, acc):
            col_start = pl.multiple_of(c * COLS, COLS)
            d2 = jnp.dot(left, packed_points_ref[:, pl.ds(col_start, COLS)], preferred_element_type=f32)
            pieces = []
            for b in range(per_tile):
                times = packed_times_ref[pl.ds(block_slot[r * per_tile + b], 1), pl.ds(col_start, COLS)]
                part = jnp.maximum(d2[b * BLOCK : (b + 1) * BLOCK], 1e-30)
                falloff = jnp.maximum(1.0 - part * lax.rsqrt(part), 0.0)
                second = falloff * falloff
                pieces.append((second * second * (5.0 * times - (4.0 * times) * falloff)).astype(bf16))
            kernel = jnp.concatenate(pieces, axis=0)
            return acc + jnp.dot(kernel, packed_weights_ref[pl.ds(col_start, COLS), :], preferred_element_type=f32)

        sums_ref[pl.ds(row_start, ROWS), :] = lax.fori_loop(
            0, col_tiles, col_step, jnp.zeros((ROWS, columns), f32)
        )
        return carry

    lax.fori_loop(0, row_tiles, row_step, 0)

    def give(g, carry):
        start = pl.multiple_of(slot_row[g] * BLOCK, BLOCK)
        partial_ref[g] = sums_ref[pl.ds(start, test_tile), :].astype(bf16)
        return carry

    lax.fori_loop(0, slots, give, 0)


def partials(narrow_id, train_counts, received, packed, slots, columns):
    test_tile = received.shape[2]
    height = slots * test_tile
    return pl.pallas_call(
        main_kernel,
        out_shape=jax.ShapeDtypeStruct((slots, test_tile, columns), bf16),
        in_specs=[SMEM, SMEM, VMEM, VMEM, VMEM, VMEM],
        out_specs=VMEM,
        scratch_shapes=[
            pltpu.VMEM((height, 48), bf16),
            pltpu.VMEM((height, columns), f32),
            pltpu.SMEM((height // BLOCK + ROWS // BLOCK,), i32),
            pltpu.SMEM((slots,), i32),
        ],
        compiler_params=pltpu.CompilerParams(vmem_limit_bytes=VMEM_LIMIT),
        cost_estimate=pl.CostEstimate(flops=3_000_000_000, bytes_accessed=4_000_000, transcendentals=8_000_000),
        name="partials",
    )(narrow_id, train_counts, received, *packed)


def collect_kernel(first_ref, owner_ref, collected_ref, out_ref):
    sources = collected_ref.shape[0]
    tiles = out_ref.shape[0]
    acc = [jnp.zeros(out_ref.shape[1:], f32) for _ in range(tiles)]
    for w in range(sources):
        block = collected_ref[w].astype(f32)
        tile = owner_ref[w] - first_ref[0]
        for t in range(tiles):
            acc[t] = acc[t] + jnp.where(tile == t, block, 0.0)
    for t in range(tiles):
        out_ref[t] = acc[t].astype(out_ref.dtype)


def collect(first, owners, collected, tiles, dtype):
    return pl.pallas_call(
        collect_kernel,
        out_shape=jax.ShapeDtypeStruct((tiles,) + collected.shape[1:], dtype),
        in_specs=[SMEM, SMEM, VMEM],
        out_specs=VMEM,
        compiler_params=pltpu.CompilerParams(vmem_limit_bytes=VMEM_LIMIT),
        cost_estimate=pl.CostEstimate(flops=1_000_000, bytes_accessed=700_000, transcendentals=0),
        name="collect",
    )(first, owners, collected)


def body(
    train_points, train_weights, train_counts, test_points, prior, test_counts, pair_count, pair_slot, slot_tile
):
    narrow_size = lax.axis_size("narrow")
    wide_size = lax.axis_size("wide")
    narrow_id = lax.axis_index("narrow")
    wide_id = lax.axis_index("wide")
    own_tests = test_points.shape[0]
    slots = slot_tile.shape[0]
    columns = train_weights.shape[2]

    wanted = lax.dynamic_index_in_dim(slot_tile, wide_id, 1, keepdims=False) - narrow_id * own_tests
    payload = jnp.concatenate(
        [
            test_points,
            jnp.broadcast_to(
                test_counts.astype(f32)[:, None, None], (own_tests, 1, test_points.shape[2])
            ),
        ],
        axis=1,
    )
    outgoing = jnp.zeros((wide_size,) + payload.shape[1:], f32)
    for t in range(own_tests):
        outgoing = jnp.where((wanted == t)[:, None, None], payload[t][None], outgoing)
    outgoing = jnp.broadcast_to(
        outgoing[:, None], (wide_size, narrow_size) + payload.shape[1:]
    ).reshape((wide_size * narrow_size,) + payload.shape[1:])
    received = lax.all_to_all(outgoing, ("wide", "narrow"), 0, 0, tiled=True)

    nid = narrow_id.astype(i32)[None]
    packed = prepare(nid, train_counts, pair_count, train_points, train_weights, pair_slot, slots)
    partial_value = partials(nid, train_counts, received, packed, slots, columns)
    collected = lax.all_to_all(partial_value, "wide", 0, 0, tiled=True)
    owners = lax.dynamic_index_in_dim(slot_tile, wide_id, 1, keepdims=False)
    arrived = []
    for k in range(1, narrow_size):
        target = lax.rem(narrow_id + k, narrow_size)
        sent = collect((target * own_tests).astype(i32)[None], owners, collected, own_tests, bf16)
        arrived.append(
            lax.ppermute(sent, "narrow", [(i, (i + k) % narrow_size) for i in range(narrow_size)])
        )
    owned = collect((narrow_id * own_tests).astype(i32)[None], owners, collected, own_tests, f32)
    for part in arrived:
        owned = owned + part.astype(f32)
    test_live = jnp.arange(prior.shape[1], dtype=i32)[None, :] < test_counts[:, None]
    update = jnp.where(test_live[:, :, None], owned, 0.0)
    return (prior.astype(f32) + update).astype(bf16)


def solution(mesh):
    return jax.shard_map(
        body,
        mesh=mesh,
        in_specs=(
            P("wide", None, None),
            P(("wide", "narrow"), None, None),
            P("wide"),
            P(("wide", "narrow"), None, None),
            P(("wide", "narrow"), None, None),
            P(("wide", "narrow")),
            P("wide"),
            P("wide", None),
            P(),
        ),
        out_specs=P(("wide", "narrow"), None, None),
        check_vma=False,
    )
```

time: 462 us -> 73.3 us (0.16)
  blocking collectives: 273 us -> 0 us
  other arithmetic: 65.5 us -> 2.37 us
  matrix products: 43.2 us -> 0 us
  local copies, waits for them, and re-layouts: 43 us -> 5.09 us
  Pallas kernels: 0 us -> 34.1 us
  between operations: 14.1 us -> 0.07 us
  waiting for transfers between devices: 12.7 us -> 18.3 us
  starting transfers between devices: 6.54 us -> 12 us
    all_to_all x1 -> x0, blocking collectives: 268 us -> none  [body(): lax.all_to_all(partial_value, 'wide', split_axis=0, concat_axis=0, tiled=...]
    dot_general x17 -> x0, matrix products: 43.2 us -> none  [the longest x15 41.9 us: block_step(): jnp.einsum('bij,bjs->bis', kernel, weights, preferred_element_type=jnp.fl...]
    scatter-add x15 -> x0, other arithmetic: 39 us -> none  [block_step(): return partial_value.at[target].add(contribution)]
    gather x60 -> x0, local copies, waits for them, and re-layouts: 38.8 us -> none  [the longest x30 17.7 us: block_step(): kernel = wendland(slot_points[target], train_points[tile_ids])]
    pallas_call x0 -> x4, Pallas kernels: none -> 34.1 us  [the longest x1 30.2 us: partials(): pl.pallas_call(main_kernel, out_shape=jax.ShapeDtypeStruct((slots, test_t...]
    all_to_all x1 -> x2, waiting for transfers between devices: 1.55 us -> 15.5 us  [the longest x1 14.5 us: body(): collected = lax.all_to_all(partial_value, 'wide', 0, 0, tiled=True)]
    select_n x46 -> x1, other arithmetic: 11.6 us -> 0.1 us  [body(): jnp.where((wanted == t)[:, None, None], payload[t][None], outgoing)]
    reduce_scatter x1 -> x0, waiting for transfers between devices: 11.1 us -> none  [body(): owned = lax.psum_scatter(grouped, 'narrow', scatter_dimension=0, tiled=True)]
  transfers between devices with their start and end apart: 2 -> 3, of which waited for: 2 -> 3; matrix products, arithmetic and copies ran while one was open for 1% -> 1% of each run, Pallas kernels for 0% -> 4%
where the time goes in v1:
time: 73.3 us; the launch traced here: 72 us
  Pallas kernels  34.1 us (47%)
  waiting for transfers between devices  18.3 us (25%)
  starting transfers between devices  12 us (16%)
  local copies, waits for them, and re-layouts  5.09 us (7%)
  other arithmetic  2.37 us (3%)
    pallas_call x1, Pallas kernels, partials(): pl.pallas_call(main_kernel, out_shape=jax.ShapeDtypeStruct((slots, test_t...  30.2 us
    all_to_all x1, waiting for transfers between devices, body(): collected = lax.all_to_all(partial_value, 'wide', 0, 0, tiled=True)  14.5 us
    all_to_all x1, starting transfers between devices, body(): received = lax.all_to_all(outgoing, ('wide', 'narrow'), 0, 0, tiled=True)  7.3 us
    unnamed x17, local copies, waits for them, and re-layouts  4.2 us
    all_to_all x1, starting transfers between devices, body(): collected = lax.all_to_all(partial_value, 'wide', 0, 0, tiled=True)  4.05 us
    ppermute x1, waiting for transfers between devices, body(): lax.ppermute(sent, 'narrow', [(i, (i + k) % narrow_size) for i in range(n...  2.79 us
    pallas_call x1, Pallas kernels, prepare(): pl.pallas_call(prepare_kernel, out_shape=(jax.ShapeDtypeStruct((length, c...  2.33 us
    pallas_call x2, Pallas kernels, collect(): pl.pallas_call(collect_kernel, out_shape=jax.ShapeDtypeStruct((tiles,) +...  1.52 us
  transfers between devices with their start and end apart: 3, of which 3 were waited for; matrix products, arithmetic and copies ran while one was open for 1% of the time, Pallas kernels for 4%

profile of v1, /device:TPU:0, one launch (start us, length us, event | category | flops | bytes accessed | tf_op | source)
XLA Modules:
  0.0 72.0 jit_solution(17314140125495911560)
XLA Ops:
  0.0 0.7 convert_element_type.13
  0.7 0.0 copy-done
  0.7 0.2 dynamic-slice_reduce_fusion.owner_ref
  0.9 0.1 broadcast_in_dim.75
  1.0 0.8 %fusion = (f32[1,4,128]{2,0,1:T(1,128)S(1)}, f32[1,4,128]{2,0,1:T(1,128)S(1)}) fusion(f32[2,1,128]{2,0,1:T(2,128)S(1)} %broadcast_in_dim.75, f32[2,3,128]{2,0,1:T(2,128)} %param.12), kind=kLoop, calls=%fused_computation.5 | loop fusion | flops 1024 | bytes 8192 | tf_op jit(solution)/shard_map/concatenate | solution.py:248
  1.7 0.1 select_select_fusion
  1.8 0.6 broadcast_in_dim.82
  2.5 7.3 %all-to-all-start = ((f32[32,4,128]{2,1,0:T(4,128)}), f32[32,4,128]{2,1,0:T(4,128)S(1)}, u32[]{:S(2)}, u32[]{:S(2)}) async-start(f32[32,4,128]{2,1,0:T(4,128)} %bitcast.4), calls=%async_computation | async-start | bytes 131072 | tf_op jit(solution)/shard_map/all_to_all | solution.py:263
  9.8 1.0 %copy.11.points_ref = f32[32,3,256]{2,1,0:T(4,128)S(1)} copy(f32[32,3,256]{2,0,1:T(8,128)} %param.9) | data formatting | bytes 196608 | tf_op args[0]
  10.8 1.2 %copy-done.1 = bf16[16,256,128]{2,1,0:T(8,128)(2,1)S(1)} copy-done((bf16[16,256,128]{2,1,0:T(8,128)(2,1)S(1)}, bf16[16,256,128]{2,1,0:T(8,128)(2,1)}, u32[]{:S(2)}) %copy-start.1) | copy-done | bytes 1048600
  12.0 0.7 copy-done.2
  12.7 0.7 copy-done.3
  13.3 0.7 copy-done.4
  14.0 2.3 %prepare.1 = (bf16[4736,128]{1,0:T(8,128)(2,1)S(1)}, bf16[48,4736]{1,0:T(8,128)(2,1)S(1)}, f32[16,4736]{1,0:T(8,128)S(1)}) custom-call(s32[1]{0:T(128)} %bitcast.1.narrow_id_ref, s32[32]{0:T(128)S(1)} %copy-done.4, s32[32]{0:T(128)S(1)} %copy-done.3, f32[32,3,256]{2,1,0:T(4,128)S(1)} %copy.11.points_ref, bf16[16,256,128]{2,1,0:T(8,128)(2,1)S(1)} %copy-done.1, ...), custom_call_target="tpu_custom_call" | custom-call | flops 40000000 | bytes 4000000 | tf_op jit(solution)/shard_map/prepare/pallas_call | solution.py:103
  16.3 1.1 %all-to-all-done.received_ref = f32[32,4,128]{2,1,0:T(4,128)S(1)} async-done(((f32[32,4,128]{2,1,0:T(4,128)}), f32[32,4,128]{2,1,0:T(4,128)S(1)}, u32[]{:S(2)}, u32[]{:S(2)}) %all-to-all-start) | async-done | bytes 65568 | tf_op jit(solution)/shard_map/all_to_all | solution.py:263
  17.4 30.2 %partials.1 = bf16[16,128,128]{2,1,0:T(8,128)(2,1)} custom-call(s32[1]{0:T(128)} %bitcast.1.narrow_id_ref, s32[32]{0:T(128)S(1)} %copy-done.5, f32[32,4,128]{2,1,0:T(4,128)S(1)} %all-to-all-done.received_ref, bf16[4736,128]{1,0:T(8,128)(2,1)S(1)} %get-tuple-element.8.packed_weights_ref, bf16[48,4736]{1,0:T(8,128)(2,1)S(1)} %get-tuple-element.9.packed_points_ref, ...), custom_call_target="tpu_custom_call" | custom-call | flops 3000000000 | bytes 4000000 | tf_op jit(solution)/shard_map/partials/pallas_call | solution.py:194
  47.6 4.1 %all-to-all-start.1 = ((bf16[16,128,128]{2,1,0:T(8,128)(2,1)}), bf16[16,128,128]{2,1,0:T(8,128)(2,1)S(1)}, u32[]{:S(2)}, u32[]{:S(2)}) async-start(bf16[16,128,128]{2,1,0:T(8,128)(2,1)} %partials.1), calls=%async_computation.1 | async-start | bytes 1048576 | tf_op jit(solution)/shard_map/all_to_all | solution.py:268
  51.7 14.5 %all-to-all-done.1.collected_ref = bf16[16,128,128]{2,1,0:T(8,128)(2,1)S(1)} async-done(((bf16[16,128,128]{2,1,0:T(8,128)(2,1)}), bf16[16,128,128]{2,1,0:T(8,128)(2,1)S(1)}, u32[]{:S(2)}, u32[]{:S(2)}) %all-to-all-start.1) | async-done | bytes 524320 | tf_op jit(solution)/shard_map/all_to_all | solution.py:268
  66.1 0.8 %collect.3 = bf16[2,128,128]{2,1,0:T(8,128)(2,1)S(1)} custom-call(s32[1]{0:T(128)} %bitcast.5.first_ref, s32[16]{0:T(128)S(1)} %dynamic-slice_reduce_fusion.owner_ref, bf16[16,128,128]{2,1,0:T(8,128)(2,1)S(1)} %all-to-all-done.1.collected_ref), custom_call_target="tpu_custom_call" | custom-call | flops 1000000 | bytes 700000 | tf_op jit(solution)/shard_map/collect/pallas_call | solution.py:225
  66.9 0.7 collective-permute-start
  67.6 0.1 iota_compare_fusion
  67.7 0.8 %collect.2 = f32[2,128,128]{2,1,0:T(8,128)S(1)} custom-call(s32[1]{0:T(128)} %bitcast.first_ref, s32[16]{0:T(128)S(1)} %dynamic-slice_reduce_fusion.owner_ref, bf16[16,128,128]{2,1,0:T(8,128)(2,1)S(1)} %all-to-all-done.1.collected_ref), custom_call_target="tpu_custom_call" | custom-call | flops 1000000 | bytes 700000 | tf_op jit(solution)/shard_map/collect/pallas_call | solution.py:225
  68.4 2.8 %collective-permute-done = bf16[2,128,128]{2,1,0:T(8,128)(2,1)S(1)} collective-permute-done((bf16[2,128,128]{2,1,0:T(8,128)(2,1)S(1)}, bf16[2,128,128]{2,1,0:T(8,128)(2,1)S(1)}, u32[]{:S(2)}, u32[]{:S(2)}) %collective-permute-start) | collective-permute-done | bytes 65568 | tf_op jit(solution)/shard_map/ppermute | solution.py:275
  71.2 0.7 %add_convert_fusion = bf16[2,128,128]{2,1,0:T(8,128)(2,1)} fusion(f32[2,128,128]{2,1,0:T(8,128)S(1)} %collect.2, bf16[2,128,128]{2,1,0:T(8,128)(2,1)S(1)} %collective-permute-done, bf16[2,128,128]{2,1,0:T(8,128)(2,1)S(1)} %copy-done.6, pred[2,128]{1,0:T(4,128)(4,1)S(1)} %iota_compare_fusion), kind=kLoop, calls=%fused_computation | loop fusion | flops 196608 | bytes 327936 | tf_op jit(solution)/shard_map/convert_element_type | solution.py:282
  (12 shorter events, 0.0 us)
Async XLA Ops:
  0.0 0.7 copy-start
  0.0 17.4 %copy-start.5 = (s32[32]{0:T(128)S(1)}, s32[32]{0:T(128)}, u32[]{:S(2)}) copy-start(s32[32]{0:T(128)} %train_counts_ref.3) | copy-start | bytes 388
  2.5 14.9 %all-to-all-start = ((f32[32,4,128]{2,1,0:T(4,128)}), f32[32,4,128]{2,1,0:T(4,128)S(1)}, u32[]{:S(2)}, u32[]{:S(2)}) async-start(f32[32,4,128]{2,1,0:T(4,128)} %bitcast.4), calls=%async_computation | async-start | bytes 131072 | tf_op jit(solution)/shard_map/all_to_all | solution.py:263
  10.7 1.2 %copy-start.1 = (bf16[16,256,128]{2,1,0:T(8,128)(2,1)S(1)}, bf16[16,256,128]{2,1,0:T(8,128)(2,1)}, u32[]{:S(2)}) copy-start(bf16[16,256,128]{2,1,0:T(8,128)(2,1)} %weights_ref.1) | copy-start | bytes 3145732
  12.0 0.7 copy-start.2
  12.7 0.7 copy-start.3
  13.3 0.7 copy-start.4
  47.6 20.0 %copy-start.7 = (s32[2]{0:T(128)S(1)}, s32[2]{0:T(128)}, u32[]{:S(2)}) copy-start(s32[2]{0:T(128)} %param.14) | copy-start | bytes 28
  47.6 23.6 %copy-start.6 = (bf16[2,128,128]{2,1,0:T(8,128)(2,1)S(1)}, bf16[2,128,128]{2,1,0:T(8,128)(2,1)}, u32[]{:S(2)}) copy-start(bf16[2,128,128]{2,1,0:T(8,128)(2,1)} %param.13) | copy-start | bytes 196612
  47.6 18.5 %all-to-all-start.1 = ((bf16[16,128,128]{2,1,0:T(8,128)(2,1)}), bf16[16,128,128]{2,1,0:T(8,128)(2,1)S(1)}, u32[]{:S(2)}, u32[]{:S(2)}) async-start(bf16[16,128,128]{2,1,0:T(8,128)(2,1)} %partials.1), calls=%async_computation.1 | async-start | bytes 1048576 | tf_op jit(solution)/shard_map/all_to_all | solution.py:268
  66.9 4.3 %collective-permute-start = (bf16[2,128,128]{2,1,0:T(8,128)(2,1)S(1)}, bf16[2,128,128]{2,1,0:T(8,128)(2,1)S(1)}, u32[]{:S(2)}, u32[]{:S(2)}) collective-permute-start(bf16[2,128,128]{2,1,0:T(8,128)(2,1)S(1)} %collect.3), channel_id=1, source_target_pairs={{0,1},{1,0},{2,3},{3,2},{4,5},{5,4},{6,7},{7,6},{8,9},{9,8},{10,11... | collective-permute-start | bytes 196616 | tf_op jit(solution)/shard_map/ppermute | solution.py:275

commit v2 on v1

v2 whole, which is shorter than its diff:
```python
import functools
import math

import jax
import jax.numpy as jnp
from jax import lax
from jax.experimental import pallas as pl
from jax.experimental.pallas import tpu as pltpu
from jax.sharding import PartitionSpec as P

f32, bf16, i32 = jnp.float32, jnp.bfloat16, jnp.int32
COLS = 256
BLOCK = 16
PART = 8
PARTS = 4
DEPTH = 256
SCALE = 4.0**0.2
VMEM_LIMIT = 48 * 1024 * 1024
VMEM = pl.BlockSpec(memory_space=pltpu.VMEM)
SMEM = pl.BlockSpec(memory_space=pltpu.SMEM)
HBM = pl.BlockSpec(memory_space=pltpu.HBM)


def split3(x):
    high = x.astype(bf16).astype(f32)
    rest = x - high
    mid = rest.astype(bf16).astype(f32)
    low = (rest - mid).astype(bf16).astype(f32)
    return high, mid, low


def stay(*arrays):
    return [pltpu.with_memory_space_constraint(array, pltpu.HBM) for array in arrays]


def offer_kernel(slot_tile_hbm, test_counts_hbm, test_points_hbm, offer_ref, slot_tile, test_counts, points, sems):
    axes, own_tests, test_tile = points.shape
    senders = offer_ref.shape[0]
    wide_size = slot_tile.shape[0]
    copies = [
        pltpu.make_async_copy(source, target, sems.at[i])
        for i, (source, target) in enumerate(
            ((slot_tile_hbm, slot_tile), (test_counts_hbm, test_counts), (test_points_hbm, points))
        )
    ]
    for copy in copies:
        copy.start()
    first = lax.axis_index("narrow") * own_tests
    group = lax.axis_index("wide")
    for copy in copies:
        copy.wait()
    payloads = [
        jnp.concatenate(
            [
                *(points[axis, t : t + 1, :] for axis in range(axes)),
                jnp.full((1, test_tile), test_counts[t].astype(f32), f32),
            ],
            axis=0,
        )
        for t in range(own_tests)
    ]
    narrow_size = senders // wide_size

    def step(w, carry):
        wanted = slot_tile[w, group] - first
        chosen = jnp.zeros((axes + 1, test_tile), f32)
        for t in range(own_tests):
            chosen = jnp.where(wanted == t, payloads[t], chosen)
        for n in range(narrow_size):
            offer_ref[w * narrow_size + n] = chosen
        return carry

    lax.fori_loop(0, wide_size, step, 0, unroll=4)


def offer(slot_tile, test_counts, test_points, senders):
    axes, own_tests, test_tile = test_points.shape
    return pl.pallas_call(
        offer_kernel,
        out_shape=jax.ShapeDtypeStruct((senders, axes + 1, test_tile), f32),
        in_specs=[HBM, HBM, HBM],
        out_specs=VMEM,
        scratch_shapes=[
            pltpu.SMEM(slot_tile.shape, i32),
            pltpu.SMEM(test_counts.shape, i32),
            pltpu.VMEM(test_points.shape, f32),
            pltpu.SemaphoreType.DMA((3,)),
        ],
        compiler_params=pltpu.CompilerParams(vmem_limit_bytes=VMEM_LIMIT),
        cost_estimate=pl.CostEstimate(flops=100_000, bytes_accessed=100_000, transcendentals=0),
        name="offer",
    )(*stay(slot_tile, test_counts, test_points))


def prepare_kernel(
    train_counts_hbm, pair_count_hbm, points_hbm, weights_hbm, pair_slot_hbm,
    packed_weights_ref, packed_points_ref, packed_times_ref,
    wide_weights, raw_points, train_counts_ref, pair_count_ref, points_ref, weights_ref, pair_slot_ref, sems,
):
    own_tiles, tile, columns = weights_ref.shape
    copies = [
        pltpu.make_async_copy(source, target, sems.at[i])
        for i, (source, target) in enumerate(
            (
                (train_counts_hbm, train_counts_ref),
                (pair_count_hbm, pair_count_ref),
                (points_hbm, points_ref),
                (weights_hbm, weights_ref),
                (pair_slot_hbm, pair_slot_ref),
            )
        )
    ]
    for copy in copies:
        copy.start()
    for copy in copies:
        copy.wait()
    slots = packed_times_ref.shape[0]
    list_length = pair_slot_ref.shape[1]
    first_tile = lax.axis_index("narrow") * own_tiles
    window = tile + 128
    positions = lax.broadcasted_iota(i32, (1, list_length), 1)
    named = pair_slot_ref[...]
    one_hot = (
        lax.broadcasted_iota(i32, (slots, list_length), 0) == jnp.broadcast_to(named, (slots, list_length))
    ).astype(f32)
    row8 = lax.broadcasted_iota(i32, (8, tile), 0)
    lane = lax.broadcasted_iota(i32, (8, window), 1)
    lane_slots = lax.broadcasted_iota(i32, (slots, window), 1)

    def skip(t, total):
        return total + pair_count_ref[t]

    first_pair = lax.fori_loop(0, first_tile, skip, jnp.int32(0))

    def step(t, carry):
        offset, pair = carry
        u = [
            SCALE * (points_ref[axis, pl.ds(first_tile + t, 1), :] - 1.0)
            for axis in range(points_ref.shape[0])
        ]
        square = u[0] * u[0] + u[1] * u[1] + u[2] * u[2]
        raw = jnp.where(row8 == 4, 1.0, 0.0)
        for row, value in enumerate((*u, square)):
            raw = jnp.where(row8 == row, value, raw)
        pair_end = pair + pair_count_ref[first_tile + t]
        inside = jnp.logical_and(positions >= pair, positions < pair_end)
        times = jnp.sum(jnp.where(inside, one_hot, 0.0), axis=1, keepdims=True)
        shift = lax.rem(offset, 128)
        base = pl.multiple_of(offset - shift, 128)
        rolled = pltpu.roll(
            jnp.concatenate([raw, jnp.zeros((8, 128), f32)], axis=1), shift, 1
        )
        spot = pl.ds(base, window)
        raw_points[:, spot] = jnp.where(lane >= shift, rolled, raw_points[:, spot])
        packed_times_ref[:, spot] = jnp.where(
            lane_slots >= shift, times, packed_times_ref[:, spot]
        )
        wide_weights[pl.ds(offset, tile), :] = weights_ref[t].astype(f32)
        return offset + train_counts_ref[first_tile + t], pair_end

    total, _ = lax.fori_loop(0, own_tiles, step, (jnp.int32(0), first_pair))
    shift = lax.rem(total, 128)
    base = pl.multiple_of(total - shift, 128)
    tail = COLS + 128
    spot = pl.ds(base, tail)
    raw_points[:, spot] = jnp.where(
        lax.broadcasted_iota(i32, (8, tail), 1) >= shift, 0.0, raw_points[:, spot]
    )
    packed_times_ref[:, spot] = jnp.where(
        lax.broadcasted_iota(i32, (slots, tail), 1) >= shift, 0.0, packed_times_ref[:, spot]
    )
    wide_weights[pl.ds(total, COLS), :] = jnp.zeros((COLS, columns), f32)

    def finish(c, carry):
        start = pl.multiple_of(c * COLS, COLS)
        high, mid, low = split3(raw_points[:, pl.ds(start, COLS)])
        packed_points_ref[:, pl.ds(start, COLS)] = jnp.concatenate(
            [high, mid, high, mid, low, high], axis=0
        ).astype(bf16)
        packed_weights_ref[pl.ds(start, COLS), :] = wide_weights[pl.ds(start, COLS), :].astype(bf16)
        return carry

    lax.fori_loop(0, (total + COLS - 1) // COLS, finish, 0)


def prepare(train_counts, pair_count, points, weights, pair_slot, slots):
    own_tiles, tile, columns = weights.shape
    length = own_tiles * tile + COLS + 128
    return pl.pallas_call(
        prepare_kernel,
        out_shape=(
            jax.ShapeDtypeStruct((length, columns), bf16),
            jax.ShapeDtypeStruct((48, length), bf16),
            jax.ShapeDtypeStruct((slots, length), f32),
        ),
        in_specs=[HBM] * 5,
        out_specs=(VMEM, VMEM, VMEM),
        scratch_shapes=[
            pltpu.VMEM((length, columns), f32),
            pltpu.VMEM((8, length), f32),
            pltpu.SMEM(train_counts.shape, i32),
            pltpu.SMEM(pair_count.shape, i32),
            pltpu.VMEM(points.shape, f32),
            pltpu.VMEM(weights.shape, bf16),
            pltpu.VMEM(pair_slot.shape, i32),
            pltpu.SemaphoreType.DMA((5,)),
        ],
        compiler_params=pltpu.CompilerParams(vmem_limit_bytes=VMEM_LIMIT),
        cost_estimate=pl.CostEstimate(flops=40_000_000, bytes_accessed=4_000_000, transcendentals=0),
        name="prepare",
    )(*stay(train_counts, pair_count, points, weights, pair_slot))


def main_kernel(
    train_counts_ref, received_ref, packed_weights_ref, packed_points_ref, packed_times_ref,
    partial_ref,
    rows_ref, sums_ref, block_slot, slot_row,
):
    slots, test_tile, columns = partial_ref.shape
    senders = received_ref.shape[0] // slots
    own_tiles = train_counts_ref.shape[0] // senders
    depth = packed_points_ref.shape[0]
    first_tile = lax.axis_index("narrow") * own_tiles
    total = lax.fori_loop(
        0, own_tiles, lambda t, a: a + train_counts_ref[first_tile + t], jnp.int32(0)
    )
    row8 = lax.broadcasted_iota(i32, (8, test_tile), 0)
    per_slot = test_tile // BLOCK
    rows_ref[...] = jnp.zeros(rows_ref.shape, bf16)
    sums_ref[...] = jnp.zeros(sums_ref.shape, f32)
    together = math.gcd(slots, 16)

    def place(step, offset):
        operands, counts = [], []
        for i in range(together):
            g = step * together + i
            got = received_ref[g * senders]
            for s in range(1, senders):
                got = got + received_ref[g * senders + s]
            counts.append(jnp.max(got[3:4, :]).astype(i32))
            v = SCALE * (jnp.concatenate([got, got], axis=0) - 1.0)
            square = jnp.sum(jnp.where(row8 < 3, v * v, 0.0), axis=0, keepdims=True)
            raw = jnp.where(
                row8 < 3, -2.0 * v, jnp.where(row8 == 3, 1.0, jnp.where(row8 == 4, square, 0.0))
            )
            high, mid, low = split3(raw)
            operands.append(
                jnp.concatenate([high, high, mid, mid, high, low], axis=0).T.astype(bf16)
            )
        for i in range(together):
            g = step * together + i
            start = pl.multiple_of(offset * BLOCK, BLOCK)
            rows_ref[pl.ds(start, test_tile), 0:depth] = operands[i]
            slot_row[g] = offset
            for b in range(per_slot):
                block_slot[offset + b] = g
            offset = offset + (counts[i] + BLOCK - 1) // BLOCK
        return offset

    blocks = lax.fori_loop(0, slots // together, place, jnp.int32(0))
    for b in range(2 * PART):
        block_slot[blocks + b] = 0
    parts = (blocks + PART - 1) // PART
    parts = jnp.where(parts < 3, 3, jnp.where(parts == 5, 6, parts))
    steps = (parts + PARTS - 1) // PARTS
    shorter = PARTS * steps - parts
    longer = steps - shorter
    col_tiles = (total + COLS - 1) // COLS
    nothing = jnp.zeros((BLOCK, DEPTH), bf16)
    ring = PARTS * PART

    def with_accumulators(*accs):
        square_accs, sum_accs = accs[: ring + 1], accs[ring + 1 :]
        for acc in accs:
            pltpu.matmul_pop(acc)

        def load_points(c):
            rows = packed_points_ref[:, pl.ds(pl.multiple_of(c * COLS, COLS), COLS)]
            pltpu.matmul_push_rhs(
                jnp.concatenate([rows, jnp.zeros((DEPTH - depth, COLS), bf16)], axis=0), 0, 0
            )
            pltpu.matmul_acc_lhs(square_accs[ring], nothing, load_staged_rhs=0)

        def load_weights(c):
            rows = packed_weights_ref[pl.ds(pl.multiple_of(c * COLS, COLS), COLS), :]
            pltpu.matmul_push_rhs(
                jnp.concatenate([rows, jnp.zeros((COLS, DEPTH - columns), bf16)], axis=1), 0, 1
            )
            pltpu.matmul_acc_lhs(sum_accs[ring], nothing, load_staged_rhs=0)

        def block_rows(part, b):
            return pl.ds(pl.multiple_of(part * (PART * BLOCK) + b * BLOCK, BLOCK), BLOCK)

        def start_squares(part, b):
            rows = rows_ref[block_rows(part, b), :]
            pltpu.matmul_acc_lhs(
                square_accs[b],
                jnp.concatenate([rows, jnp.zeros((BLOCK, DEPTH - rows.shape[1]), bf16)], axis=1),
            )

        def gather_sums(part, b):
            rows = block_rows(part, b)
            sums_ref[rows, :] = sums_ref[rows, :] + pltpu.matmul_pop(sum_accs[b])[:, :columns]

        def evaluate(c, part, count, after, before):
            col = pl.ds(pl.multiple_of(c * COLS, COLS), COLS)
            for b in range(ring):
                square = pltpu.matmul_pop(square_accs[b])
                start_squares(after, b)
                gather_sums(before, b)
                if b < count * PART:
                    square = jnp.maximum(square, 1e-30)
                    times = packed_times_ref[pl.ds(block_slot[part * PART + b], 1), col]
                    falloff = jnp.maximum(SCALE - square * lax.rsqrt(square), 0.0)
                    second = falloff * falloff
                    kernel = (second * second * (1.25 * SCALE - falloff) * times).astype(bf16)
                    pltpu.matmul_acc_lhs(sum_accs[b], kernel)

        def last_step(c, before, count):
            load_points(c + 1)
            evaluate(c, parts - count, count, 0, before)
            load_weights(c + 1)

        def col_step(c, before):
            def long_step(q, before):
                part = PARTS * q
                evaluate(c, part, PARTS, part + PARTS, before)
                return part

            def short_step(q, before):
                part = PARTS * longer + (PARTS - 1) * q
                evaluate(c, part, PARTS - 1, part + (PARTS - 1), before)
                return part

            before = lax.fori_loop(0, longer - (shorter == 0).astype(i32), long_step, before)
            before = lax.fori_loop(0, shorter - 1, short_step, before)
            pl.when(shorter == 0)(functools.partial(last_step, c, before, PARTS))
            pl.when(shorter > 0)(functools.partial(last_step, c, before, PARTS - 1))
            return parts - jnp.where(shorter == 0, PARTS, PARTS - 1)

        load_points(jnp.int32(0))
        load_weights(jnp.int32(0))
        for b in range(ring):
            start_squares(jnp.int32(0), b)
        before = lax.fori_loop(0, col_tiles, col_step, jnp.int32(0))
        for b in range(ring):
            gather_sums(before, b)
            pltpu.matmul_pop(square_accs[b])
        pltpu.matmul_pop(square_accs[ring])
        pltpu.matmul_pop(sum_accs[ring])

    pl.run_scoped(
        with_accumulators,
        *[pltpu.ACC(mxu)((BLOCK, DEPTH), f32) for mxu in range(2) for _ in range(ring + 1)],
    )

    def give(step, carry):
        for i in range(together):
            g = step * together + i
            start = pl.multiple_of(slot_row[g] * BLOCK, BLOCK)
            partial_ref[g] = sums_ref[pl.ds(start, test_tile), :].astype(bf16)
        return carry

    lax.fori_loop(0, slots // together, give, 0)


def partials(train_counts, received, packed, slots, columns):
    test_tile = received.shape[2]
    step_rows = PARTS * PART * BLOCK
    height = max(slots * test_tile, 6 * PART * BLOCK) + step_rows
    return pl.pallas_call(
        main_kernel,
        out_shape=jax.ShapeDtypeStruct((slots, test_tile, columns), bf16),
        in_specs=[SMEM, VMEM, VMEM, VMEM, VMEM],
        out_specs=VMEM,
        scratch_shapes=[
            pltpu.VMEM((height, 128), bf16),
            pltpu.VMEM((height, columns), f32),
            pltpu.SMEM((height // BLOCK,), i32),
            pltpu.SMEM((slots,), i32),
        ],
        compiler_params=pltpu.CompilerParams(vmem_limit_bytes=VMEM_LIMIT),
        cost_estimate=pl.CostEstimate(flops=3_000_000_000, bytes_accessed=4_000_000, transcendentals=8_000_000),
        name="partials",
    )(train_counts, received, *packed)


def collect_kernel(shift, slot_tile_ref, collected_ref, out_ref):
    sources = collected_ref.shape[0]
    tiles = out_ref.shape[0]
    group = lax.axis_index("wide")
    first = lax.rem(lax.axis_index("narrow") + shift, lax.axis_size("narrow")) * tiles
    acc = [jnp.zeros(out_ref.shape[1:], f32) for _ in range(tiles)]
    for w in range(sources):
        block = collected_ref[w].astype(f32)
        tile = slot_tile_ref[w, group] - first
        for t in range(tiles):
            acc[t] = acc[t] + jnp.where(tile == t, block, 0.0)
    for t in range(tiles):
        out_ref[t] = acc[t].astype(out_ref.dtype)


def collect(shift, slot_tile, collected, tiles, dtype):
    return pl.pallas_call(
        functools.partial(collect_kernel, shift),
        out_shape=jax.ShapeDtypeStruct((tiles,) + collected.shape[1:], dtype),
        in_specs=[SMEM, VMEM],
        out_specs=VMEM,
        compiler_params=pltpu.CompilerParams(vmem_limit_bytes=VMEM_LIMIT),
        cost_estimate=pl.CostEstimate(flops=1_000_000, bytes_accessed=700_000, transcendentals=0),
        name="collect",
    )(slot_tile, collected)


def body(
    train_points, train_weights, train_counts, test_points, prior, test_counts, pair_count, pair_slot, slot_tile
):
    narrow_size = lax.axis_size("narrow")
    own_tests = test_points.shape[0]
    slots = slot_tile.shape[0]
    columns = train_weights.shape[2]
    offered = offer(slot_tile, test_counts, jnp.transpose(test_points, (1, 0, 2)), slots * narrow_size)
    received = lax.all_to_all(offered, ("wide", "narrow"), 0, 0, tiled=True)
    packed = prepare(
        train_counts, pair_count, jnp.transpose(train_points, (1, 0, 2)), train_weights, pair_slot, slots
    )
    partial_value = partials(train_counts, received, packed, slots, columns)
    collected = lax.all_to_all(partial_value, "wide", 0, 0, tiled=True)
    arrived = []
    for k in range(1, narrow_size):
        sent = collect(k, slot_tile, collected, own_tests, bf16)
        arrived.append(
            lax.ppermute(sent, "narrow", [(i, (i + k) % narrow_size) for i in range(narrow_size)])
        )
    owned = collect(0, slot_tile, collected, own_tests, f32)
    for part in arrived:
        owned = owned + part.astype(f32)
    test_live = jnp.arange(prior.shape[1], dtype=i32)[None, :] < test_counts[:, None]
    update = jnp.where(test_live[:, :, None], owned, 0.0)
    return (prior.astype(f32) + update).astype(bf16)


def solution(mesh):
    return jax.shard_map(
        body,
        mesh=mesh,
        in_specs=(
            P("wide", None, None),
            P(("wide", "narrow"), None, None),
            P("wide"),
            P(("wide", "narrow"), None, None),
            P(("wide", "narrow"), None, None),
            P(("wide", "narrow")),
            P("wide"),
            P("wide", None),
            P(),
        ),
        out_specs=P(("wide", "narrow"), None, None),
        check_vma=False,
    )
```

time: 73.3 us -> 48.6 us (0.66); the launches traced: 72 us -> 48.4 us
  Pallas kernels: 34.1 us -> 14.9 us
  blocking collectives: 0 us -> 17.5 us
  waiting for transfers between devices: 18.3 us -> 5.72 us
  local copies, waits for them, and re-layouts: 5.09 us -> 0.02 us
  starting transfers between devices: 12 us -> 9.4 us
  other arithmetic: 2.37 us -> 0.81 us
    pallas_call x1, Pallas kernels: 30.2 us -> 8.27 us  [partials(): pl.pallas_call(main_kernel, out_shape=jax.ShapeDtypeStruct((slots, test_t...]
    all_to_all x0 -> x1, blocking collectives: none -> 17.5 us  [body(): collected = lax.all_to_all(partial_value, 'wide', 0, 0, tiled=True)]
    all_to_all x2 -> x1, waiting for transfers between devices: 15.5 us -> 4.42 us  [body(): received = lax.all_to_all(offered, ('wide', 'narrow'), 0, 0, tiled=True)]
    unnamed x17 -> x8, local copies, waits for them, and re-layouts: 4.2 us -> 0.02 us
    all_to_all x2 -> x1, starting transfers between devices: 11.3 us -> 7.3 us  [body(): received = lax.all_to_all(offered, ('wide', 'narrow'), 0, 0, tiled=True)]
    pallas_call x2 -> x3, Pallas kernels: 1.52 us -> 3.45 us  [the longest x2 1.79 us: collect(): pl.pallas_call(functools.partial(collect_kernel, shift), out_shape=jax.Sh...]
    ppermute x1, waiting for transfers between devices: 2.79 us -> 1.3 us  [body(): lax.ppermute(sent, 'narrow', [(i, (i + k) % narrow_size) for i in range(n...]
    ppermute x1, starting transfers between devices: 0.7 us -> 2.1 us  [body(): lax.ppermute(sent, 'narrow', [(i, (i + k) % narrow_size) for i in range(n...]
  transfers between devices with their start and end apart: 3 -> 2, of which waited for: 3 -> 2; matrix products, arithmetic and copies ran while one was open for 1% -> 0% of each run, Pallas kernels for 4% -> 8%
where the time goes in v2:
time: 48.6 us; the launch traced here: 48.4 us
  blocking collectives  17.5 us (36%)
  Pallas kernels  14.9 us (31%)
  starting transfers between devices  9.4 us (19%)
  waiting for transfers between devices  5.72 us (12%)
  other arithmetic  0.81 us (2%)
    all_to_all x1, blocking collectives, body(): collected = lax.all_to_all(partial_value, 'wide', 0, 0, tiled=True)  17.5 us
    pallas_call x1, Pallas kernels, partials(): pl.pallas_call(main_kernel, out_shape=jax.ShapeDtypeStruct((slots, test_t...  8.27 us
    all_to_all x1, starting transfers between devices, body(): received = lax.all_to_all(offered, ('wide', 'narrow'), 0, 0, tiled=True)  7.3 us
    all_to_all x1, waiting for transfers between devices, body(): received = lax.all_to_all(offered, ('wide', 'narrow'), 0, 0, tiled=True)  4.42 us
    pallas_call x1, Pallas kernels, prepare(): pl.pallas_call(prepare_kernel, out_shape=(jax.ShapeDtypeStruct((length, c...  3.17 us
    ppermute x1, starting transfers between devices, body(): lax.ppermute(sent, 'narrow', [(i, (i + k) % narrow_size) for i in range(n...  2.1 us
    pallas_call x2, Pallas kernels, collect(): pl.pallas_call(functools.partial(collect_kernel, shift), out_shape=jax.Sh...  1.79 us
    pallas_call x1, Pallas kernels, offer(): pl.pallas_call(offer_kernel, out_shape=jax.ShapeDtypeStruct((senders, axe...  1.66 us
  transfers between devices with their start and end apart: 2, of which 2 were waited for; matrix products, arithmetic and copies ran while one was open for 0% of the time, Pallas kernels for 8%

profile of v2, /device:TPU:0, one launch (start us, length us, event | category | flops | bytes accessed | tf_op | source)
XLA Modules:
  0.0 48.4 jit_solution(7945976216642027456)
XLA Ops:
  0.0 0.0 copy-start.1
  0.0 1.7 %offer.1 = f32[32,4,128]{2,1,0:T(4,128)} custom-call(s32[16,16]{1,0:T(8,128)} %slot_tile_ref.3, s32[2]{0:T(128)} %test_counts_hbm.1, f32[3,2,128]{2,1,0:T(2,128)} %bitcast.3), custom_call_target="tpu_custom_call" | custom-call | flops 100000 | bytes 100000 | tf_op jit(solution)/shard_map/offer/pallas_call | solution.py:78
  1.7 7.3 %all-to-all-start = ((f32[32,4,128]{2,1,0:T(4,128)}), f32[32,4,128]{2,1,0:T(4,128)S(1)}, u32[]{:S(2)}, u32[]{:S(2)}) async-start(f32[32,4,128]{2,1,0:T(4,128)} %offer.1), calls=%async_computation | async-start | bytes 131072 | tf_op jit(solution)/shard_map/all_to_all | solution.py:423
  9.0 3.2 %prepare.1 = (bf16[4480,128]{1,0:T(8,128)(2,1)S(1)}, bf16[48,4480]{1,0:T(8,128)(2,1)S(1)}, f32[16,4480]{1,0:T(8,128)S(1)}) custom-call(s32[32]{0:T(128)} %train_counts_ref.1, s32[32]{0:T(128)} %pair_count_hbm.1, f32[3,32,256]{2,1,0:T(8,128)} %bitcast.2, bf16[16,256,128]{2,1,0:T(8,128)(2,1)} %weights_hbm.1, s32[1,1280]{1,0:T(1,128)} %pair_slot_hbm.1), custom_call_target="tpu_custom_call" | custom-call | flops 40000000 | bytes 4000000 | tf_op jit(solution)/shard_map/prepare/pallas_call | solution.py:189
  12.2 4.4 %all-to-all-done.received_ref = f32[32,4,128]{2,1,0:T(4,128)S(1)} async-done(((f32[32,4,128]{2,1,0:T(4,128)}), f32[32,4,128]{2,1,0:T(4,128)S(1)}, u32[]{:S(2)}, u32[]{:S(2)}) %all-to-all-start) | async-done | bytes 65568 | tf_op jit(solution)/shard_map/all_to_all | solution.py:423
  16.6 0.0 copy-done.1
  16.6 0.0 copy-start
  16.6 8.3 %partials.1 = bf16[16,128,128]{2,1,0:T(8,128)(2,1)S(1)} custom-call(s32[32]{0:T(128)S(1)} %copy-done.1, f32[32,4,128]{2,1,0:T(4,128)S(1)} %all-to-all-done.received_ref, bf16[4480,128]{1,0:T(8,128)(2,1)S(1)} %get-tuple-element.8.packed_weights_ref, bf16[48,4480]{1,0:T(8,128)(2,1)S(1)} %get-tuple-element.9.packed_points_ref, ...), custom_call_target="tpu_custom_call" | custom-call | flops 3000000000 | bytes 4000000 | tf_op jit(solution)/shard_map/partials/pallas_call | solution.py:371
  24.9 0.0 copy-start.3
  24.9 0.0 copy-start.2
  24.9 17.5 %all_to_all.10.collected_ref = bf16[16,128,128]{2,1,0:T(8,128)(2,1)S(1)} all-to-all(bf16[16,128,128]{2,1,0:T(8,128)(2,1)S(1)} %partials.1), channel_id=1, replica_groups=mesh['wide'=16,'narrow'=2] {'wide'}, dimensions={0} | all-to-all | bytes 1048576 | tf_op jit(solution)/shard_map/all_to_all | solution.py:428
  42.4 0.0 copy-done
  42.4 0.9 %collect.3 = bf16[2,128,128]{2,1,0:T(8,128)(2,1)S(1)} custom-call(s32[16,16]{1,0:T(8,128)S(1)} %copy-done, bf16[16,128,128]{2,1,0:T(8,128)(2,1)S(1)} %all_to_all.10.collected_ref), custom_call_target="tpu_custom_call" | custom-call | flops 1000000 | bytes 700000 | tf_op jit(solution)/shard_map/collect/pallas_call | solution.py:404
  43.3 2.1 %collective-permute-start = (bf16[2,128,128]{2,1,0:T(8,128)(2,1)S(1)}, bf16[2,128,128]{2,1,0:T(8,128)(2,1)S(1)}, u32[]{:S(2)}, u32[]{:S(2)}) collective-permute-start(bf16[2,128,128]{2,1,0:T(8,128)(2,1)S(1)} %collect.3), channel_id=1, source_target_pairs={{0,1},{1,0},{2,3},{3,2},{4,5},{5,4},{6,7},{7,6},{8,9},{9,8},{10,11... | collective-permute-start | bytes 196616 | tf_op jit(solution)/shard_map/ppermute | solution.py:433
  45.4 0.0 copy-done.3
  45.4 0.1 iota_compare_fusion
  45.5 0.9 %collect.2 = f32[2,128,128]{2,1,0:T(8,128)S(1)} custom-call(s32[16,16]{1,0:T(8,128)S(1)} %copy-done, bf16[16,128,128]{2,1,0:T(8,128)(2,1)S(1)} %all_to_all.10.collected_ref), custom_call_target="tpu_custom_call" | custom-call | flops 1000000 | bytes 700000 | tf_op jit(solution)/shard_map/collect/pallas_call | solution.py:404
  46.4 1.3 %collective-permute-done = bf16[2,128,128]{2,1,0:T(8,128)(2,1)S(1)} collective-permute-done((bf16[2,128,128]{2,1,0:T(8,128)(2,1)S(1)}, bf16[2,128,128]{2,1,0:T(8,128)(2,1)S(1)}, u32[]{:S(2)}, u32[]{:S(2)}) %collective-permute-start) | collective-permute-done | bytes 65568 | tf_op jit(solution)/shard_map/ppermute | solution.py:433
  47.7 0.0 copy-done.2
  47.7 0.7 %add_convert_fusion = bf16[2,128,128]{2,1,0:T(8,128)(2,1)} fusion(f32[2,128,128]{2,1,0:T(8,128)S(1)} %collect.2, bf16[2,128,128]{2,1,0:T(8,128)(2,1)S(1)} %collective-permute-done, bf16[2,128,128]{2,1,0:T(8,128)(2,1)S(1)} %copy-done.2, pred[2,128]{1,0:T(4,128)(4,1)S(1)} %iota_compare_fusion), kind=kLoop, calls=%fused_computation | loop fusion | flops 196608 | bytes 327936 | tf_op jit(solution)/shard_map/convert_element_type | solution.py:440
Async XLA Ops:
  0.0 16.6 %copy-start.1 = (s32[32]{0:T(128)S(1)}, s32[32]{0:T(128)}, u32[]{:S(2)}) copy-start(s32[32]{0:T(128)} %train_counts_ref.1) | copy-start | bytes 388
  1.7 14.9 %all-to-all-start = ((f32[32,4,128]{2,1,0:T(4,128)}), f32[32,4,128]{2,1,0:T(4,128)S(1)}, u32[]{:S(2)}, u32[]{:S(2)}) async-start(f32[32,4,128]{2,1,0:T(4,128)} %offer.1), calls=%async_computation | async-start | bytes 131072 | tf_op jit(solution)/shard_map/all_to_all | solution.py:423
  16.6 25.8 %copy-start = (s32[16,16]{1,0:T(8,128)S(1)}, s32[16,16]{1,0:T(8,128)}, u32[]{:S(2)}) copy-start(s32[16,16]{1,0:T(8,128)} %slot_tile_ref.3) | copy-start | bytes 3076
  24.9 20.6 %copy-start.3 = (s32[2]{0:T(128)S(1)}, s32[2]{0:T(128)}, u32[]{:S(2)}) copy-start(s32[2]{0:T(128)} %test_counts_hbm.1) | copy-start | bytes 28
  24.9 22.8 %copy-start.2 = (bf16[2,128,128]{2,1,0:T(8,128)(2,1)S(1)}, bf16[2,128,128]{2,1,0:T(8,128)(2,1)}, u32[]{:S(2)}) copy-start(bf16[2,128,128]{2,1,0:T(8,128)(2,1)} %param.13) | copy-start | bytes 196612
  43.3 4.4 %collective-permute-start = (bf16[2,128,128]{2,1,0:T(8,128)(2,1)S(1)}, bf16[2,128,128]{2,1,0:T(8,128)(2,1)S(1)}, u32[]{:S(2)}, u32[]{:S(2)}) collective-permute-start(bf16[2,128,128]{2,1,0:T(8,128)(2,1)S(1)} %collect.3), channel_id=1, source_target_pairs={{0,1},{1,0},{2,3},{3,2},{4,5},{5,4},{6,7},{7,6},{8,9},{9,8},{10,11... | collective-permute-start | bytes 196616 | tf_op jit(solution)/shard_map/ppermute | solution.py:433

commit v3 on v2

--- a/solution.py
+++ b/solution.py
@@ -15,7 +15,7 @@
 PARTS = 4
 DEPTH = 256
 SCALE = 4.0**0.2
-VMEM_LIMIT = 48 * 1024 * 1024
+VMEM_LIMIT = 32 * 1024 * 1024
 VMEM = pl.BlockSpec(memory_space=pltpu.VMEM)
 SMEM = pl.BlockSpec(memory_space=pltpu.SMEM)
 HBM = pl.BlockSpec(memory_space=pltpu.HBM)
@@ -212,21 +212,18 @@
 
 
 def main_kernel(
-    train_counts_ref, received_ref, packed_weights_ref, packed_points_ref, packed_times_ref,
+    train_counts_hbm, received_ref, packed_weights_ref, packed_points_ref, packed_times_ref,
     partial_ref,
-    rows_ref, sums_ref, block_slot, slot_row,
+    rows_ref, sums_ref, block_slot, slot_row, train_counts_ref, sem,
 ):
+    fetch = pltpu.make_async_copy(train_counts_hbm, train_counts_ref, sem)
+    fetch.start()
     slots, test_tile, columns = partial_ref.shape
     senders = received_ref.shape[0] // slots
     own_tiles = train_counts_ref.shape[0] // senders
     depth = packed_points_ref.shape[0]
-    first_tile = lax.axis_index("narrow") * own_tiles
-    total = lax.fori_loop(
-        0, own_tiles, lambda t, a: a + train_counts_ref[first_tile + t], jnp.int32(0)
-    )
     row8 = lax.broadcasted_iota(i32, (8, test_tile), 0)
     per_slot = test_tile // BLOCK
-    rows_ref[...] = jnp.zeros(rows_ref.shape, bf16)
     sums_ref[...] = jnp.zeros(sums_ref.shape, f32)
     together = math.gcd(slots, 16)
 
@@ -244,13 +241,13 @@
                 row8 < 3, -2.0 * v, jnp.where(row8 == 3, 1.0, jnp.where(row8 == 4, square, 0.0))
             )
             high, mid, low = split3(raw)
-            operands.append(
-                jnp.concatenate([high, high, mid, mid, high, low], axis=0).T.astype(bf16)
-            )
+            operand = jnp.concatenate([high, high, mid, mid, high, low], axis=0).T
+            lanes = jnp.zeros((test_tile, rows_ref.shape[1] - depth), f32)
+            operands.append(jnp.concatenate([operand, lanes], axis=1).astype(bf16))
         for i in range(together):
             g = step * together + i
             start = pl.multiple_of(offset * BLOCK, BLOCK)
-            rows_ref[pl.ds(start, test_tile), 0:depth] = operands[i]
+            rows_ref[pl.ds(start, test_tile), :] = operands[i]
             slot_row[g] = offset
             for b in range(per_slot):
                 block_slot[offset + b] = g
@@ -258,6 +255,11 @@
         return offset
 
     blocks = lax.fori_loop(0, slots // together, place, jnp.int32(0))
+    fetch.wait()
+    first_tile = lax.axis_index("narrow") * own_tiles
+    total = lax.fori_loop(
+        0, own_tiles, lambda t, a: a + train_counts_ref[first_tile + t], jnp.int32(0)
+    )
     for b in range(2 * PART):
         block_slot[blocks + b] = 0
     parts = (blocks + PART - 1) // PART
@@ -274,18 +276,22 @@
         for acc in accs:
             pltpu.matmul_pop(acc)
 
-        def load_points(c):
+        def push_points(c):
             rows = packed_points_ref[:, pl.ds(pl.multiple_of(c * COLS, COLS), COLS)]
             pltpu.matmul_push_rhs(
                 jnp.concatenate([rows, jnp.zeros((DEPTH - depth, COLS), bf16)], axis=0), 0, 0
             )
+
+        def take_points():
             pltpu.matmul_acc_lhs(square_accs[ring], nothing, load_staged_rhs=0)
 
-        def load_weights(c):
+        def push_weights(c):
             rows = packed_weights_ref[pl.ds(pl.multiple_of(c * COLS, COLS), COLS), :]
             pltpu.matmul_push_rhs(
                 jnp.concatenate([rows, jnp.zeros((COLS, DEPTH - columns), bf16)], axis=1), 0, 1
             )
+
+        def take_weights():
             pltpu.matmul_acc_lhs(sum_accs[ring], nothing, load_staged_rhs=0)
 
         def block_rows(part, b):
@@ -317,9 +323,11 @@
                     pltpu.matmul_acc_lhs(sum_accs[b], kernel)
 
         def last_step(c, before, count):
-            load_points(c + 1)
+            take_points()
+            push_weights(c + 1)
             evaluate(c, parts - count, count, 0, before)
-            load_weights(c + 1)
+            take_weights()
+            push_points(jnp.minimum(c + 2, col_tiles))
 
         def col_step(c, before):
             def long_step(q, before):
@@ -338,14 +346,18 @@
             pl.when(shorter > 0)(functools.partial(last_step, c, before, PARTS - 1))
             return parts - jnp.where(shorter == 0, PARTS, PARTS - 1)
 
-        load_points(jnp.int32(0))
-        load_weights(jnp.int32(0))
+        push_points(jnp.int32(0))
+        take_points()
+        push_points(jnp.int32(1))
+        push_weights(jnp.int32(0))
+        take_weights()
         for b in range(ring):
             start_squares(jnp.int32(0), b)
         before = lax.fori_loop(0, col_tiles, col_step, jnp.int32(0))
         for b in range(ring):
             gather_sums(before, b)
             pltpu.matmul_pop(square_accs[b])
+        take_points()
         pltpu.matmul_pop(square_accs[ring])
         pltpu.matmul_pop(sum_accs[ring])
 
@@ -371,18 +383,20 @@
     return pl.pallas_call(
         main_kernel,
         out_shape=jax.ShapeDtypeStruct((slots, test_tile, columns), bf16),
-        in_specs=[SMEM, VMEM, VMEM, VMEM, VMEM],
+        in_specs=[HBM, VMEM, VMEM, VMEM, VMEM],
         out_specs=VMEM,
         scratch_shapes=[
             pltpu.VMEM((height, 128), bf16),
             pltpu.VMEM((height, columns), f32),
             pltpu.SMEM((height // BLOCK,), i32),
             pltpu.SMEM((slots,), i32),
+            pltpu.SMEM(train_counts.shape, i32),
+            pltpu.SemaphoreType.DMA(()),
         ],
         compiler_params=pltpu.CompilerParams(vmem_limit_bytes=VMEM_LIMIT),
         cost_estimate=pl.CostEstimate(flops=3_000_000_000, bytes_accessed=4_000_000, transcendentals=8_000_000),
         name="partials",
-    )(train_counts, received, *packed)
+    )(*stay(train_counts), received, *packed)
 
 
 def collect_kernel(shift, slot_tile_ref, collected_ref, out_ref):

time: 48.6 us -> 48.9 us (level)
  starting transfers between devices: 9.4 us -> 7.67 us
  waiting for transfers between devices: 5.72 us -> 7.38 us
  Pallas kernels: 14.9 us -> 15.7 us
    ppermute x1, starting transfers between devices: 2.1 us -> 0.37 us  [body(): lax.ppermute(sent, 'narrow', [(i, (i + k) % narrow_size) for i in range(n...]
    ppermute x1, waiting for transfers between devices: 1.3 us -> 2.99 us  [body(): lax.ppermute(sent, 'narrow', [(i, (i + k) % narrow_size) for i in range(n...]
    pallas_call x1, Pallas kernels: 8.27 us -> 9.14 us  [partials(): pl.pallas_call(main_kernel, out_shape=jax.ShapeDtypeStruct((slots, test_t...]
where the time goes in v3:
time: 48.9 us; the launch traced here: 48.8 us
  blocking collectives  17.2 us (35%)
  Pallas kernels  15.7 us (32%)
  starting transfers between devices  7.67 us (16%)
  waiting for transfers between devices  7.38 us (15%)
  other arithmetic  0.81 us (2%)
    all_to_all x1, blocking collectives, body(): collected = lax.all_to_all(partial_value, 'wide', 0, 0, tiled=True)  17.2 us
    pallas_call x1, Pallas kernels, partials(): pl.pallas_call(main_kernel, out_shape=jax.ShapeDtypeStruct((slots, test_t...  9.14 us
    all_to_all x1, starting transfers between devices, body(): received = lax.all_to_all(offered, ('wide', 'narrow'), 0, 0, tiled=True)  7.3 us
    all_to_all x1, waiting for transfers between devices, body(): received = lax.all_to_all(offered, ('wide', 'narrow'), 0, 0, tiled=True)  4.4 us
    pallas_call x1, Pallas kernels, prepare(): pl.pallas_call(prepare_kernel, out_shape=(jax.ShapeDtypeStruct((length, c...  3.2 us
    ppermute x1, waiting for transfers between devices, body(): lax.ppermute(sent, 'narrow', [(i, (i + k) % narrow_size) for i in range(n...  2.99 us
    pallas_call x2, Pallas kernels, collect(): pl.pallas_call(functools.partial(collect_kernel, shift), out_shape=jax.Sh...  1.79 us
    pallas_call x1, Pallas kernels, offer(): pl.pallas_call(offer_kernel, out_shape=jax.ShapeDtypeStruct((senders, axe...  1.53 us
  transfers between devices with their start and end apart: 2, of which 2 were waited for; matrix products, arithmetic and copies ran while one was open for 0% of the time, Pallas kernels for 8%

profile of v3, /device:TPU:0, one launch (start us, length us, event | category | flops | bytes accessed | tf_op | source)
XLA Modules:
  0.0 48.8 jit_solution(1677711020797866269)
XLA Ops:
  0.0 1.5 %offer.1 = f32[32,4,128]{2,1,0:T(4,128)} custom-call(s32[16,16]{1,0:T(8,128)} %slot_tile_ref.3, s32[2]{0:T(128)} %test_counts_hbm.1, f32[3,2,128]{2,1,0:T(2,128)} %bitcast.3), custom_call_target="tpu_custom_call" | custom-call | flops 100000 | bytes 100000 | tf_op jit(solution)/shard_map/offer/pallas_call | solution.py:78
  1.5 7.3 %all-to-all-start = ((f32[32,4,128]{2,1,0:T(4,128)}), f32[32,4,128]{2,1,0:T(4,128)S(1)}, u32[]{:S(2)}, u32[]{:S(2)}) async-start(f32[32,4,128]{2,1,0:T(4,128)} %offer.1), calls=%async_computation | async-start | bytes 131072 | tf_op jit(solution)/shard_map/all_to_all | solution.py:437
  8.8 3.2 %prepare.1 = (bf16[4480,128]{1,0:T(8,128)(2,1)S(1)}, bf16[48,4480]{1,0:T(8,128)(2,1)S(1)}, f32[16,4480]{1,0:T(8,128)S(1)}) custom-call(s32[32]{0:T(128)} %train_counts_hbm.3, s32[32]{0:T(128)} %pair_count_hbm.1, f32[3,32,256]{2,1,0:T(8,128)} %bitcast.2, bf16[16,256,128]{2,1,0:T(8,128)(2,1)} %weights_hbm.1, s32[1,1280]{1,0:T(1,128)} %pair_slot_hbm.1), custom_call_target="tpu_custom_call" | custom-call | flops 40000000 | bytes 4000000 | tf_op jit(solution)/shard_map/prepare/pallas_call | solution.py:189
  12.1 4.4 %all-to-all-done.received_ref = f32[32,4,128]{2,1,0:T(4,128)S(1)} async-done(((f32[32,4,128]{2,1,0:T(4,128)}), f32[32,4,128]{2,1,0:T(4,128)S(1)}, u32[]{:S(2)}, u32[]{:S(2)}) %all-to-all-start) | async-done | bytes 65568 | tf_op jit(solution)/shard_map/all_to_all | solution.py:437
  16.5 0.0 copy-start
  16.5 9.1 %partials.1 = bf16[16,128,128]{2,1,0:T(8,128)(2,1)S(1)} custom-call(s32[32]{0:T(128)} %train_counts_hbm.3, f32[32,4,128]{2,1,0:T(4,128)S(1)} %all-to-all-done.received_ref, bf16[4480,128]{1,0:T(8,128)(2,1)S(1)} %get-tuple-element.8.packed_weights_ref, bf16[48,4480]{1,0:T(8,128)(2,1)S(1)} %get-tuple-element.9.packed_points_ref, ...), custom_call_target="tpu_custom_call" | custom-call | flops 3000000000 | bytes 4000000 | tf_op jit(solution)/shard_map/partials/pallas_call | solution.py:383
  25.6 0.0 copy-start.2
  25.6 0.0 copy-start.1
  25.6 17.2 %all_to_all.10.collected_ref = bf16[16,128,128]{2,1,0:T(8,128)(2,1)S(1)} all-to-all(bf16[16,128,128]{2,1,0:T(8,128)(2,1)S(1)} %partials.1), channel_id=1, replica_groups=mesh['wide'=16,'narrow'=2] {'wide'}, dimensions={0} | all-to-all | bytes 1048576 | tf_op jit(solution)/shard_map/all_to_all | solution.py:442
  42.8 0.0 copy-done
  42.8 0.9 %collect.3 = bf16[2,128,128]{2,1,0:T(8,128)(2,1)S(1)} custom-call(s32[16,16]{1,0:T(8,128)S(1)} %copy-done, bf16[16,128,128]{2,1,0:T(8,128)(2,1)S(1)} %all_to_all.10.collected_ref), custom_call_target="tpu_custom_call" | custom-call | flops 1000000 | bytes 700000 | tf_op jit(solution)/shard_map/collect/pallas_call | solution.py:418
  43.7 0.4 collective-permute-start
  44.1 0.0 copy-done.2
  44.1 0.1 iota_compare_fusion
  44.2 0.9 %collect.2 = f32[2,128,128]{2,1,0:T(8,128)S(1)} custom-call(s32[16,16]{1,0:T(8,128)S(1)} %copy-done, bf16[16,128,128]{2,1,0:T(8,128)(2,1)S(1)} %all_to_all.10.collected_ref), custom_call_target="tpu_custom_call" | custom-call | flops 1000000 | bytes 700000 | tf_op jit(solution)/shard_map/collect/pallas_call | solution.py:418
  45.1 3.0 %collective-permute-done = bf16[2,128,128]{2,1,0:T(8,128)(2,1)S(1)} collective-permute-done((bf16[2,128,128]{2,1,0:T(8,128)(2,1)S(1)}, bf16[2,128,128]{2,1,0:T(8,128)(2,1)S(1)}, u32[]{:S(2)}, u32[]{:S(2)}) %collective-permute-start) | collective-permute-done | bytes 65568 | tf_op jit(solution)/shard_map/ppermute | solution.py:447
  48.1 0.0 copy-done.1
  48.1 0.7 %add_convert_fusion = bf16[2,128,128]{2,1,0:T(8,128)(2,1)} fusion(f32[2,128,128]{2,1,0:T(8,128)S(1)} %collect.2, bf16[2,128,128]{2,1,0:T(8,128)(2,1)S(1)} %collective-permute-done, bf16[2,128,128]{2,1,0:T(8,128)(2,1)S(1)} %copy-done.1, pred[2,128]{1,0:T(4,128)(4,1)S(1)} %iota_compare_fusion), kind=kLoop, calls=%fused_computation | loop fusion | flops 196608 | bytes 327936 | tf_op jit(solution)/shard_map/convert_element_type | solution.py:454
Async XLA Ops:
  1.5 14.9 %all-to-all-start = ((f32[32,4,128]{2,1,0:T(4,128)}), f32[32,4,128]{2,1,0:T(4,128)S(1)}, u32[]{:S(2)}, u32[]{:S(2)}) async-start(f32[32,4,128]{2,1,0:T(4,128)} %offer.1), calls=%async_computation | async-start | bytes 131072 | tf_op jit(solution)/shard_map/all_to_all | solution.py:437
  16.5 26.4 %copy-start = (s32[16,16]{1,0:T(8,128)S(1)}, s32[16,16]{1,0:T(8,128)}, u32[]{:S(2)}) copy-start(s32[16,16]{1,0:T(8,128)} %slot_tile_ref.3) | copy-start | bytes 3076
  25.6 18.5 %copy-start.2 = (s32[2]{0:T(128)S(1)}, s32[2]{0:T(128)}, u32[]{:S(2)}) copy-start(s32[2]{0:T(128)} %test_counts_hbm.1) | copy-start | bytes 28
  25.6 22.5 %copy-start.1 = (bf16[2,128,128]{2,1,0:T(8,128)(2,1)S(1)}, bf16[2,128,128]{2,1,0:T(8,128)(2,1)}, u32[]{:S(2)}) copy-start(bf16[2,128,128]{2,1,0:T(8,128)(2,1)} %param.13) | copy-start | bytes 196612
  43.7 4.3 %collective-permute-start = (bf16[2,128,128]{2,1,0:T(8,128)(2,1)S(1)}, bf16[2,128,128]{2,1,0:T(8,128)(2,1)S(1)}, u32[]{:S(2)}, u32[]{:S(2)}) collective-permute-start(bf16[2,128,128]{2,1,0:T(8,128)(2,1)S(1)} %collect.3), channel_id=1, source_target_pairs={{0,1},{1,0},{2,3},{3,2},{4,5},{5,4},{6,7},{7,6},{8,9},{9,8},{10,11... | collective-permute-start | bytes 196616 | tf_op jit(solution)/shard_map/ppermute | solution.py:447

commit v4 on v3

--- a/solution.py
+++ b/solution.py
@@ -399,19 +399,18 @@
     )(*stay(train_counts), received, *packed)
 
 
-def collect_kernel(shift, slot_tile_ref, collected_ref, out_ref):
+def collect_kernel(shift, slot_tile_ref, collected_ref, out_ref, sums_ref):
     sources = collected_ref.shape[0]
     tiles = out_ref.shape[0]
     group = lax.axis_index("wide")
     first = lax.rem(lax.axis_index("narrow") + shift, lax.axis_size("narrow")) * tiles
-    acc = [jnp.zeros(out_ref.shape[1:], f32) for _ in range(tiles)]
+    sums_ref[...] = jnp.zeros(sums_ref.shape, f32)
     for w in range(sources):
-        block = collected_ref[w].astype(f32)
         tile = slot_tile_ref[w, group] - first
-        for t in range(tiles):
-            acc[t] = acc[t] + jnp.where(tile == t, block, 0.0)
+        spot = jnp.where(jnp.logical_and(tile >= 0, tile < tiles), tile, tiles)
+        sums_ref[spot] = sums_ref[spot] + collected_ref[w].astype(f32)
     for t in range(tiles):
-        out_ref[t] = acc[t].astype(out_ref.dtype)
+        out_ref[t] = sums_ref[t].astype(out_ref.dtype)
 
 
 def collect(shift, slot_tile, collected, tiles, dtype):
@@ -420,6 +419,7 @@
         out_shape=jax.ShapeDtypeStruct((tiles,) + collected.shape[1:], dtype),
         in_specs=[SMEM, VMEM],
         out_specs=VMEM,
+        scratch_shapes=[pltpu.VMEM((tiles + 1,) + collected.shape[1:], f32)],
         compiler_params=pltpu.CompilerParams(vmem_limit_bytes=VMEM_LIMIT),
         cost_estimate=pl.CostEstimate(flops=1_000_000, bytes_accessed=700_000, transcendentals=0),
         name="collect",

time: 48.9 us -> 49.4 us (1.010)
  Pallas kernels: 15.7 us -> 16.2 us
    pallas_call x1, Pallas kernels: 9.14 us -> 9.84 us  [partials(): pl.pallas_call(main_kernel, out_shape=jax.ShapeDtypeStruct((slots, test_t...]
where the time goes in v4:
time: 49.4 us
  blocking collectives  17.2 us (35%)
  Pallas kernels  16.2 us (33%)
  starting transfers between devices  7.66 us (16%)
  waiting for transfers between devices  7.46 us (15%)
  other arithmetic  0.81 us (2%)
    all_to_all x1, blocking collectives, body(): collected = lax.all_to_all(partial_value, 'wide', 0, 0, tiled=True)  17.2 us
    pallas_call x1, Pallas kernels, partials(): pl.pallas_call(main_kernel, out_shape=jax.ShapeDtypeStruct((slots, test_t...  9.84 us
    all_to_all x1, starting transfers between devices, body(): received = lax.all_to_all(offered, ('wide', 'narrow'), 0, 0, tiled=True)  7.3 us
    all_to_all x1, waiting for transfers between devices, body(): received = lax.all_to_all(offered, ('wide', 'narrow'), 0, 0, tiled=True)  4.39 us
    pallas_call x1, Pallas kernels, prepare(): pl.pallas_call(prepare_kernel, out_shape=(jax.ShapeDtypeStruct((length, c...  3.21 us
    ppermute x1, waiting for transfers between devices, body(): lax.ppermute(sent, 'narrow', [(i, (i + k) % narrow_size) for i in range(n...  3.07 us
    pallas_call x2, Pallas kernels, collect(): pl.pallas_call(functools.partial(collect_kernel, shift), out_shape=jax.Sh...  1.64 us
    pallas_call x1, Pallas kernels, offer(): pl.pallas_call(offer_kernel, out_shape=jax.ShapeDtypeStruct((senders, axe...  1.53 us
  transfers between devices with their start and end apart: 2, of which 2 were waited for; matrix products, arithmetic and copies ran while one was open for 0% of the time, Pallas kernels for 8%

profile of v4, /device:TPU:0, one launch (start us, length us, event | category | flops | bytes accessed | tf_op | source)
XLA Modules:
  0.0 49.4 jit_solution(12514547512437836917)
XLA Ops:
  0.0 1.5 %offer.1 = f32[32,4,128]{2,1,0:T(4,128)} custom-call(s32[16,16]{1,0:T(8,128)} %slot_tile_ref.3, s32[2]{0:T(128)} %test_counts_hbm.1, f32[3,2,128]{2,1,0:T(2,128)} %bitcast.3), custom_call_target="tpu_custom_call" | custom-call | flops 100000 | bytes 100000 | tf_op jit(solution)/shard_map/offer/pallas_call | solution.py:78
  1.5 7.3 %all-to-all-start = ((f32[32,4,128]{2,1,0:T(4,128)}), f32[32,4,128]{2,1,0:T(4,128)S(1)}, u32[]{:S(2)}, u32[]{:S(2)}) async-start(f32[32,4,128]{2,1,0:T(4,128)} %offer.1), calls=%async_computation | async-start | bytes 131072 | tf_op jit(solution)/shard_map/all_to_all | solution.py:437
  8.8 3.2 %prepare.1 = (bf16[4480,128]{1,0:T(8,128)(2,1)S(1)}, bf16[48,4480]{1,0:T(8,128)(2,1)S(1)}, f32[16,4480]{1,0:T(8,128)S(1)}) custom-call(s32[32]{0:T(128)} %train_counts_hbm.3, s32[32]{0:T(128)} %pair_count_hbm.1, f32[3,32,256]{2,1,0:T(8,128)} %bitcast.2, bf16[16,256,128]{2,1,0:T(8,128)(2,1)} %weights_hbm.1, s32[1,1280]{1,0:T(1,128)} %pair_slot_hbm.1), custom_call_target="tpu_custom_call" | custom-call | flops 40000000 | bytes 4000000 | tf_op jit(solution)/shard_map/prepare/pallas_call | solution.py:189
  12.1 4.4 %all-to-all-done.received_ref = f32[32,4,128]{2,1,0:T(4,128)S(1)} async-done(((f32[32,4,128]{2,1,0:T(4,128)}), f32[32,4,128]{2,1,0:T(4,128)S(1)}, u32[]{:S(2)}, u32[]{:S(2)}) %all-to-all-start) | async-done | bytes 65568 | tf_op jit(solution)/shard_map/all_to_all | solution.py:437
  16.5 0.0 copy-start
  16.5 9.8 %partials.1 = bf16[16,128,128]{2,1,0:T(8,128)(2,1)S(1)} custom-call(s32[32]{0:T(128)} %train_counts_hbm.3, f32[32,4,128]{2,1,0:T(4,128)S(1)} %all-to-all-done.received_ref, bf16[4480,128]{1,0:T(8,128)(2,1)S(1)} %get-tuple-element.8.packed_weights_ref, bf16[48,4480]{1,0:T(8,128)(2,1)S(1)} %get-tuple-element.9.packed_points_ref, ...), custom_call_target="tpu_custom_call" | custom-call | flops 3000000000 | bytes 4000000 | tf_op jit(solution)/shard_map/partials/pallas_call | solution.py:383
  26.3 0.0 copy-start.2
  26.3 0.0 copy-start.1
  26.3 17.2 %all_to_all.10.collected_ref = bf16[16,128,128]{2,1,0:T(8,128)(2,1)S(1)} all-to-all(bf16[16,128,128]{2,1,0:T(8,128)(2,1)S(1)} %partials.1), channel_id=1, replica_groups=mesh['wide'=16,'narrow'=2] {'wide'}, dimensions={0} | all-to-all | bytes 1048576 | tf_op jit(solution)/shard_map/all_to_all | solution.py:442
  43.5 0.0 copy-done
  43.5 0.8 %collect.3 = bf16[2,128,128]{2,1,0:T(8,128)(2,1)S(1)} custom-call(s32[16,16]{1,0:T(8,128)S(1)} %copy-done, bf16[16,128,128]{2,1,0:T(8,128)(2,1)S(1)} %all_to_all.10.collected_ref), custom_call_target="tpu_custom_call" | custom-call | flops 1000000 | bytes 700000 | tf_op jit(solution)/shard_map/collect/pallas_call | solution.py:417
  44.4 0.4 collective-permute-start
  44.7 0.0 copy-done.2
  44.7 0.1 iota_compare_fusion
  44.8 0.8 %collect.2 = f32[2,128,128]{2,1,0:T(8,128)S(1)} custom-call(s32[16,16]{1,0:T(8,128)S(1)} %copy-done, bf16[16,128,128]{2,1,0:T(8,128)(2,1)S(1)} %all_to_all.10.collected_ref), custom_call_target="tpu_custom_call" | custom-call | flops 1000000 | bytes 700000 | tf_op jit(solution)/shard_map/collect/pallas_call | solution.py:417
  45.6 3.1 %collective-permute-done = bf16[2,128,128]{2,1,0:T(8,128)(2,1)S(1)} collective-permute-done((bf16[2,128,128]{2,1,0:T(8,128)(2,1)S(1)}, bf16[2,128,128]{2,1,0:T(8,128)(2,1)S(1)}, u32[]{:S(2)}, u32[]{:S(2)}) %collective-permute-start) | collective-permute-done | bytes 65568 | tf_op jit(solution)/shard_map/ppermute | solution.py:447
  48.7 0.0 copy-done.1
  48.7 0.7 %add_convert_fusion = bf16[2,128,128]{2,1,0:T(8,128)(2,1)} fusion(f32[2,128,128]{2,1,0:T(8,128)S(1)} %collect.2, bf16[2,128,128]{2,1,0:T(8,128)(2,1)S(1)} %collective-permute-done, bf16[2,128,128]{2,1,0:T(8,128)(2,1)S(1)} %copy-done.1, pred[2,128]{1,0:T(4,128)(4,1)S(1)} %iota_compare_fusion), kind=kLoop, calls=%fused_computation | loop fusion | flops 196608 | bytes 327936 | tf_op jit(solution)/shard_map/convert_element_type | solution.py:454
Async XLA Ops:
  1.5 14.9 %all-to-all-start = ((f32[32,4,128]{2,1,0:T(4,128)}), f32[32,4,128]{2,1,0:T(4,128)S(1)}, u32[]{:S(2)}, u32[]{:S(2)}) async-start(f32[32,4,128]{2,1,0:T(4,128)} %offer.1), calls=%async_computation | async-start | bytes 131072 | tf_op jit(solution)/shard_map/all_to_all | solution.py:437
  16.5 27.1 %copy-start = (s32[16,16]{1,0:T(8,128)S(1)}, s32[16,16]{1,0:T(8,128)}, u32[]{:S(2)}) copy-start(s32[16,16]{1,0:T(8,128)} %slot_tile_ref.3) | copy-start | bytes 3076
  26.3 18.4 %copy-start.2 = (s32[2]{0:T(128)S(1)}, s32[2]{0:T(128)}, u32[]{:S(2)}) copy-start(s32[2]{0:T(128)} %test_counts_hbm.1) | copy-start | bytes 28
  26.3 22.4 %copy-start.1 = (bf16[2,128,128]{2,1,0:T(8,128)(2,1)S(1)}, bf16[2,128,128]{2,1,0:T(8,128)(2,1)}, u32[]{:S(2)}) copy-start(bf16[2,128,128]{2,1,0:T(8,128)(2,1)} %param.13) | copy-start | bytes 196612
  44.4 4.3 %collective-permute-start = (bf16[2,128,128]{2,1,0:T(8,128)(2,1)S(1)}, bf16[2,128,128]{2,1,0:T(8,128)(2,1)S(1)}, u32[]{:S(2)}, u32[]{:S(2)}) collective-permute-start(bf16[2,128,128]{2,1,0:T(8,128)(2,1)S(1)} %collect.3), channel_id=1, source_target_pairs={{0,1},{1,0},{2,3},{3,2},{4,5},{5,4},{6,7},{7,6},{8,9},{9,8},{10,11... | collective-permute-start | bytes 196616 | tf_op jit(solution)/shard_map/ppermute | solution.py:447

commit v5 on v4

--- a/solution.py
+++ b/solution.py
@@ -224,7 +224,8 @@
     depth = packed_points_ref.shape[0]
     row8 = lax.broadcasted_iota(i32, (8, test_tile), 0)
     per_slot = test_tile // BLOCK
-    sums_ref[...] = jnp.zeros(sums_ref.shape, f32)
+    early = sums_ref.shape[0] * 3 // 10 // BLOCK * BLOCK
+    sums_ref[:early, :] = jnp.zeros((early, columns), f32)
     together = math.gcd(slots, 16)
 
     def place(step, offset):
@@ -241,9 +242,10 @@
                 row8 < 3, -2.0 * v, jnp.where(row8 == 3, 1.0, jnp.where(row8 == 4, square, 0.0))
             )
             high, mid, low = split3(raw)
-            operand = jnp.concatenate([high, high, mid, mid, high, low], axis=0).T
-            lanes = jnp.zeros((test_tile, rows_ref.shape[1] - depth), f32)
-            operands.append(jnp.concatenate([operand, lanes], axis=1).astype(bf16))
+            spare = jnp.zeros((rows_ref.shape[1] - depth, test_tile), f32)
+            operands.append(
+                jnp.concatenate([high, high, mid, mid, high, low, spare], axis=0).astype(bf16).T
+            )
         for i in range(together):
             g = step * together + i
             start = pl.multiple_of(offset * BLOCK, BLOCK)
@@ -275,6 +277,8 @@
         square_accs, sum_accs = accs[: ring + 1], accs[ring + 1 :]
         for acc in accs:
             pltpu.matmul_pop(acc)
+        late = sums_ref.shape[0] - early
+        sums_ref[early:, :] = jnp.zeros((late, columns), f32)
 
         def push_points(c):
             rows = packed_points_ref[:, pl.ds(pl.multiple_of(c * COLS, COLS), COLS)]

time: 49.4 us -> 48.4 us (0.980)
  Pallas kernels: 16.2 us -> 14.8 us
  starting transfers between devices: 7.66 us -> 8.45 us
  waiting for transfers between devices: 7.46 us -> 6.69 us
    pallas_call x1, Pallas kernels: 9.84 us -> 8.46 us  [partials(): pl.pallas_call(main_kernel, out_shape=jax.ShapeDtypeStruct((slots, test_t...]
    ppermute x1, starting transfers between devices: 0.35 us -> 1.15 us  [body(): lax.ppermute(sent, 'narrow', [(i, (i + k) % narrow_size) for i in range(n...]
    ppermute x1, waiting for transfers between devices: 3.07 us -> 2.28 us  [body(): lax.ppermute(sent, 'narrow', [(i, (i + k) % narrow_size) for i in range(n...]
where the time goes in v5:
time: 48.4 us; the launch traced here: 48.1 us
  blocking collectives  17.2 us (36%)
  Pallas kernels  14.8 us (31%)
  starting transfers between devices  8.45 us (17%)
  waiting for transfers between devices  6.69 us (14%)
  other arithmetic  0.81 us (2%)
    all_to_all x1, blocking collectives, body(): collected = lax.all_to_all(partial_value, 'wide', 0, 0, tiled=True)  17.2 us
    pallas_call x1, Pallas kernels, partials(): pl.pallas_call(main_kernel, out_shape=jax.ShapeDtypeStruct((slots, test_t...  8.46 us
    all_to_all x1, starting transfers between devices, body(): received = lax.all_to_all(offered, ('wide', 'narrow'), 0, 0, tiled=True)  7.3 us
    all_to_all x1, waiting for transfers between devices, body(): received = lax.all_to_all(offered, ('wide', 'narrow'), 0, 0, tiled=True)  4.41 us
    pallas_call x1, Pallas kernels, prepare(): pl.pallas_call(prepare_kernel, out_shape=(jax.ShapeDtypeStruct((length, c...  3.19 us
    ppermute x1, waiting for transfers between devices, body(): lax.ppermute(sent, 'narrow', [(i, (i + k) % narrow_size) for i in range(n...  2.28 us
    pallas_call x2, Pallas kernels, collect(): pl.pallas_call(functools.partial(collect_kernel, shift), out_shape=jax.Sh...  1.64 us
    pallas_call x1, Pallas kernels, offer(): pl.pallas_call(offer_kernel, out_shape=jax.ShapeDtypeStruct((senders, axe...  1.53 us
  transfers between devices with their start and end apart: 2, of which 2 were waited for; matrix products, arithmetic and copies ran while one was open for 0% of the time, Pallas kernels for 8%

profile of v5, /device:TPU:0, one launch (start us, length us, event | category | flops | bytes accessed | tf_op | source)
XLA Modules:
  0.0 48.1 jit_solution(13673842914821275816)
XLA Ops:
  0.0 1.5 %offer.1 = f32[32,4,128]{2,1,0:T(4,128)} custom-call(s32[16,16]{1,0:T(8,128)} %slot_tile_ref.3, s32[2]{0:T(128)} %test_counts_hbm.1, f32[3,2,128]{2,1,0:T(2,128)} %bitcast.3), custom_call_target="tpu_custom_call" | custom-call | flops 100000 | bytes 100000 | tf_op jit(solution)/shard_map/offer/pallas_call | solution.py:78
  1.5 7.3 %all-to-all-start = ((f32[32,4,128]{2,1,0:T(4,128)}), f32[32,4,128]{2,1,0:T(4,128)S(1)}, u32[]{:S(2)}, u32[]{:S(2)}) async-start(f32[32,4,128]{2,1,0:T(4,128)} %offer.1), calls=%async_computation | async-start | bytes 131072 | tf_op jit(solution)/shard_map/all_to_all | solution.py:441
  8.8 3.2 %prepare.1 = (bf16[4480,128]{1,0:T(8,128)(2,1)S(1)}, bf16[48,4480]{1,0:T(8,128)(2,1)S(1)}, f32[16,4480]{1,0:T(8,128)S(1)}) custom-call(s32[32]{0:T(128)} %train_counts_hbm.3, s32[32]{0:T(128)} %pair_count_hbm.1, f32[3,32,256]{2,1,0:T(8,128)} %bitcast.2, bf16[16,256,128]{2,1,0:T(8,128)(2,1)} %weights_hbm.1, s32[1,1280]{1,0:T(1,128)} %pair_slot_hbm.1), custom_call_target="tpu_custom_call" | custom-call | flops 40000000 | bytes 4000000 | tf_op jit(solution)/shard_map/prepare/pallas_call | solution.py:189
  12.0 4.4 %all-to-all-done.received_ref = f32[32,4,128]{2,1,0:T(4,128)S(1)} async-done(((f32[32,4,128]{2,1,0:T(4,128)}), f32[32,4,128]{2,1,0:T(4,128)S(1)}, u32[]{:S(2)}, u32[]{:S(2)}) %all-to-all-start) | async-done | bytes 65568 | tf_op jit(solution)/shard_map/all_to_all | solution.py:441
  16.5 0.0 copy-start
  16.5 8.5 %partials.1 = bf16[16,128,128]{2,1,0:T(8,128)(2,1)S(1)} custom-call(s32[32]{0:T(128)} %train_counts_hbm.3, f32[32,4,128]{2,1,0:T(4,128)S(1)} %all-to-all-done.received_ref, bf16[4480,128]{1,0:T(8,128)(2,1)S(1)} %get-tuple-element.8.packed_weights_ref, bf16[48,4480]{1,0:T(8,128)(2,1)S(1)} %get-tuple-element.9.packed_points_ref, ...), custom_call_target="tpu_custom_call" | custom-call | flops 3000000000 | bytes 4000000 | tf_op jit(solution)/shard_map/partials/pallas_call | solution.py:387
  24.9 0.0 copy-start.2
  24.9 0.0 copy-start.1
  25.0 17.2 %all_to_all.10.collected_ref = bf16[16,128,128]{2,1,0:T(8,128)(2,1)S(1)} all-to-all(bf16[16,128,128]{2,1,0:T(8,128)(2,1)S(1)} %partials.1), channel_id=1, replica_groups=mesh['wide'=16,'narrow'=2] {'wide'}, dimensions={0} | all-to-all | bytes 1048576 | tf_op jit(solution)/shard_map/all_to_all | solution.py:446
  42.2 0.0 copy-done
  42.2 0.8 %collect.3 = bf16[2,128,128]{2,1,0:T(8,128)(2,1)S(1)} custom-call(s32[16,16]{1,0:T(8,128)S(1)} %copy-done, bf16[16,128,128]{2,1,0:T(8,128)(2,1)S(1)} %all_to_all.10.collected_ref), custom_call_target="tpu_custom_call" | custom-call | flops 1000000 | bytes 700000 | tf_op jit(solution)/shard_map/collect/pallas_call | solution.py:421
  43.0 1.1 %collective-permute-start = (bf16[2,128,128]{2,1,0:T(8,128)(2,1)S(1)}, bf16[2,128,128]{2,1,0:T(8,128)(2,1)S(1)}, u32[]{:S(2)}, u32[]{:S(2)}) collective-permute-start(bf16[2,128,128]{2,1,0:T(8,128)(2,1)S(1)} %collect.3), channel_id=1, source_target_pairs={{0,1},{1,0},{2,3},{3,2},{4,5},{5,4},{6,7},{7,6},{8,9},{9,8},{10,11... | collective-permute-start | bytes 196616 | tf_op jit(solution)/shard_map/ppermute | solution.py:451
  44.1 0.0 copy-done.2
  44.1 0.1 iota_compare_fusion
  44.2 0.8 %collect.2 = f32[2,128,128]{2,1,0:T(8,128)S(1)} custom-call(s32[16,16]{1,0:T(8,128)S(1)} %copy-done, bf16[16,128,128]{2,1,0:T(8,128)(2,1)S(1)} %all_to_all.10.collected_ref), custom_call_target="tpu_custom_call" | custom-call | flops 1000000 | bytes 700000 | tf_op jit(solution)/shard_map/collect/pallas_call | solution.py:421
  45.0 2.3 %collective-permute-done = bf16[2,128,128]{2,1,0:T(8,128)(2,1)S(1)} collective-permute-done((bf16[2,128,128]{2,1,0:T(8,128)(2,1)S(1)}, bf16[2,128,128]{2,1,0:T(8,128)(2,1)S(1)}, u32[]{:S(2)}, u32[]{:S(2)}) %collective-permute-start) | collective-permute-done | bytes 65568 | tf_op jit(solution)/shard_map/ppermute | solution.py:451
  47.3 0.0 copy-done.1
  47.3 0.7 %add_convert_fusion = bf16[2,128,128]{2,1,0:T(8,128)(2,1)} fusion(f32[2,128,128]{2,1,0:T(8,128)S(1)} %collect.2, bf16[2,128,128]{2,1,0:T(8,128)(2,1)S(1)} %collective-permute-done, bf16[2,128,128]{2,1,0:T(8,128)(2,1)S(1)} %copy-done.1, pred[2,128]{1,0:T(4,128)(4,1)S(1)} %iota_compare_fusion), kind=kLoop, calls=%fused_computation | loop fusion | flops 196608 | bytes 327936 | tf_op jit(solution)/shard_map/convert_element_type | solution.py:458
Async XLA Ops:
  1.5 14.9 %all-to-all-start = ((f32[32,4,128]{2,1,0:T(4,128)}), f32[32,4,128]{2,1,0:T(4,128)S(1)}, u32[]{:S(2)}, u32[]{:S(2)}) async-start(f32[32,4,128]{2,1,0:T(4,128)} %offer.1), calls=%async_computation | async-start | bytes 131072 | tf_op jit(solution)/shard_map/all_to_all | solution.py:441
  16.5 25.7 %copy-start = (s32[16,16]{1,0:T(8,128)S(1)}, s32[16,16]{1,0:T(8,128)}, u32[]{:S(2)}) copy-start(s32[16,16]{1,0:T(8,128)} %slot_tile_ref.3) | copy-start | bytes 3076
  24.9 19.2 %copy-start.2 = (s32[2]{0:T(128)S(1)}, s32[2]{0:T(128)}, u32[]{:S(2)}) copy-start(s32[2]{0:T(128)} %test_counts_hbm.1) | copy-start | bytes 28
  24.9 22.4 %copy-start.1 = (bf16[2,128,128]{2,1,0:T(8,128)(2,1)S(1)}, bf16[2,128,128]{2,1,0:T(8,128)(2,1)}, u32[]{:S(2)}) copy-start(bf16[2,128,128]{2,1,0:T(8,128)(2,1)} %param.13) | copy-start | bytes 196612
  43.0 4.3 %collective-permute-start = (bf16[2,128,128]{2,1,0:T(8,128)(2,1)S(1)}, bf16[2,128,128]{2,1,0:T(8,128)(2,1)S(1)}, u32[]{:S(2)}, u32[]{:S(2)}) collective-permute-start(bf16[2,128,128]{2,1,0:T(8,128)(2,1)S(1)} %collect.3), channel_id=1, source_target_pairs={{0,1},{1,0},{2,3},{3,2},{4,5},{5,4},{6,7},{7,6},{8,9},{9,8},{10,11... | collective-permute-start | bytes 196616 | tf_op jit(solution)/shard_map/ppermute | solution.py:451

commit v6 on v4

--- a/solution.py
+++ b/solution.py
@@ -47,8 +47,8 @@
         copy.start()
     first = lax.axis_index("narrow") * own_tests
     group = lax.axis_index("wide")
-    for copy in copies:
-        copy.wait()
+    copies[1].wait()
+    copies[2].wait()
     payloads = [
         jnp.concatenate(
             [
@@ -60,6 +60,7 @@
         for t in range(own_tests)
     ]
     narrow_size = senders // wide_size
+    copies[0].wait()
 
     def step(w, carry):
         wanted = slot_tile[w, group] - first
@@ -70,7 +71,7 @@
             offer_ref[w * narrow_size + n] = chosen
         return carry
 
-    lax.fori_loop(0, wide_size, step, 0, unroll=4)
+    lax.fori_loop(0, wide_size, step, 0, unroll=16)
 
 
 def offer(slot_tile, test_counts, test_points, senders):
@@ -234,9 +235,9 @@
             got = received_ref[g * senders]
             for s in range(1, senders):
                 got = got + received_ref[g * senders + s]
-            counts.append(jnp.max(got[3:4, :]).astype(i32))
+            counts.append(got[3, 0].astype(i32))
             v = SCALE * (jnp.concatenate([got, got], axis=0) - 1.0)
-            square = jnp.sum(jnp.where(row8 < 3, v * v, 0.0), axis=0, keepdims=True)
+            square = v[0:1] * v[0:1] + v[1:2] * v[1:2] + v[2:3] * v[2:3]
             raw = jnp.where(
                 row8 < 3, -2.0 * v, jnp.where(row8 == 3, 1.0, jnp.where(row8 == 4, square, 0.0))
             )

time: 49.4 us -> 48.5 us (0.982)
  Pallas kernels: 16.2 us -> 14.1 us
  blocking collectives: 17.2 us -> 18.3 us
  starting transfers between devices: 7.66 us -> 8.24 us
  waiting for transfers between devices: 7.46 us -> 6.9 us
    pallas_call x1, Pallas kernels: 9.84 us -> 7.8 us  [partials(): pl.pallas_call(main_kernel, out_shape=jax.ShapeDtypeStruct((slots, test_t...]
    all_to_all x1, blocking collectives: 17.2 us -> 18.3 us  [body(): collected = lax.all_to_all(partial_value, 'wide', 0, 0, tiled=True)]
    ppermute x1, starting transfers between devices: 0.35 us -> 0.94 us  [body(): lax.ppermute(sent, 'narrow', [(i, (i + k) % narrow_size) for i in range(n...]
    ppermute x1, waiting for transfers between devices: 3.07 us -> 2.49 us  [body(): lax.ppermute(sent, 'narrow', [(i, (i + k) % narrow_size) for i in range(n...]
where the time goes in v6:
time: 48.5 us; the launch traced here: 48.4 us
  blocking collectives  18.3 us (38%)
  Pallas kernels  14.1 us (29%)
  starting transfers between devices  8.24 us (17%)
  waiting for transfers between devices  6.9 us (14%)
  other arithmetic  0.81 us (2%)
    all_to_all x1, blocking collectives, body(): collected = lax.all_to_all(partial_value, 'wide', 0, 0, tiled=True)  18.3 us
    pallas_call x1, Pallas kernels, partials(): pl.pallas_call(main_kernel, out_shape=jax.ShapeDtypeStruct((slots, test_t...  7.8 us
    all_to_all x1, starting transfers between devices, body(): received = lax.all_to_all(offered, ('wide', 'narrow'), 0, 0, tiled=True)  7.3 us
    all_to_all x1, waiting for transfers between devices, body(): received = lax.all_to_all(offered, ('wide', 'narrow'), 0, 0, tiled=True)  4.41 us
    pallas_call x1, Pallas kernels, prepare(): pl.pallas_call(prepare_kernel, out_shape=(jax.ShapeDtypeStruct((length, c...  3.19 us
    ppermute x1, waiting for transfers between devices, body(): lax.ppermute(sent, 'narrow', [(i, (i + k) % narrow_size) for i in range(n...  2.49 us
    pallas_call x2, Pallas kernels, collect(): pl.pallas_call(functools.partial(collect_kernel, shift), out_shape=jax.Sh...  1.65 us
    pallas_call x1, Pallas kernels, offer(): pl.pallas_call(offer_kernel, out_shape=jax.ShapeDtypeStruct((senders, axe...  1.51 us
  transfers between devices with their start and end apart: 2, of which 2 were waited for; matrix products, arithmetic and copies ran while one was open for 0% of the time, Pallas kernels for 8%

profile of v6, /device:TPU:0, one launch (start us, length us, event | category | flops | bytes accessed | tf_op | source)
XLA Modules:
  0.0 48.4 jit_solution(6181753665902739152)
XLA Ops:
  0.0 1.5 %offer.1 = f32[32,4,128]{2,1,0:T(4,128)} custom-call(s32[16,16]{1,0:T(8,128)} %slot_tile_ref.3, s32[2]{0:T(128)} %test_counts_hbm.1, f32[3,2,128]{2,1,0:T(2,128)} %bitcast.3), custom_call_target="tpu_custom_call" | custom-call | flops 100000 | bytes 100000 | tf_op jit(solution)/shard_map/offer/pallas_call | solution.py:79
  1.5 7.3 %all-to-all-start = ((f32[32,4,128]{2,1,0:T(4,128)}), f32[32,4,128]{2,1,0:T(4,128)S(1)}, u32[]{:S(2)}, u32[]{:S(2)}) async-start(f32[32,4,128]{2,1,0:T(4,128)} %offer.1), calls=%async_computation | async-start | bytes 131072 | tf_op jit(solution)/shard_map/all_to_all | solution.py:438
  8.8 3.2 %prepare.1 = (bf16[4480,128]{1,0:T(8,128)(2,1)S(1)}, bf16[48,4480]{1,0:T(8,128)(2,1)S(1)}, f32[16,4480]{1,0:T(8,128)S(1)}) custom-call(s32[32]{0:T(128)} %train_counts_hbm.3, s32[32]{0:T(128)} %pair_count_hbm.1, f32[3,32,256]{2,1,0:T(8,128)} %bitcast.2, bf16[16,256,128]{2,1,0:T(8,128)(2,1)} %weights_hbm.1, s32[1,1280]{1,0:T(1,128)} %pair_slot_hbm.1), custom_call_target="tpu_custom_call" | custom-call | flops 40000000 | bytes 4000000 | tf_op jit(solution)/shard_map/prepare/pallas_call | solution.py:190
  12.0 4.4 %all-to-all-done.received_ref = f32[32,4,128]{2,1,0:T(4,128)S(1)} async-done(((f32[32,4,128]{2,1,0:T(4,128)}), f32[32,4,128]{2,1,0:T(4,128)S(1)}, u32[]{:S(2)}, u32[]{:S(2)}) %all-to-all-start) | async-done | bytes 65568 | tf_op jit(solution)/shard_map/all_to_all | solution.py:438
  16.4 0.0 copy-start
  16.4 7.8 %partials.1 = bf16[16,128,128]{2,1,0:T(8,128)(2,1)S(1)} custom-call(s32[32]{0:T(128)} %train_counts_hbm.3, f32[32,4,128]{2,1,0:T(4,128)S(1)} %all-to-all-done.received_ref, bf16[4480,128]{1,0:T(8,128)(2,1)S(1)} %get-tuple-element.8.packed_weights_ref, bf16[48,4480]{1,0:T(8,128)(2,1)S(1)} %get-tuple-element.9.packed_points_ref, ...), custom_call_target="tpu_custom_call" | custom-call | flops 3000000000 | bytes 4000000 | tf_op jit(solution)/shard_map/partials/pallas_call | solution.py:384
  24.2 0.0 copy-start.2
  24.3 0.0 copy-start.1
  24.3 18.3 %all_to_all.10.collected_ref = bf16[16,128,128]{2,1,0:T(8,128)(2,1)S(1)} all-to-all(bf16[16,128,128]{2,1,0:T(8,128)(2,1)S(1)} %partials.1), channel_id=1, replica_groups=mesh['wide'=16,'narrow'=2] {'wide'}, dimensions={0} | all-to-all | bytes 1048576 | tf_op jit(solution)/shard_map/all_to_all | solution.py:443
  42.5 0.0 copy-done
  42.5 0.8 %collect.3 = bf16[2,128,128]{2,1,0:T(8,128)(2,1)S(1)} custom-call(s32[16,16]{1,0:T(8,128)S(1)} %copy-done, bf16[16,128,128]{2,1,0:T(8,128)(2,1)S(1)} %all_to_all.10.collected_ref), custom_call_target="tpu_custom_call" | custom-call | flops 1000000 | bytes 700000 | tf_op jit(solution)/shard_map/collect/pallas_call | solution.py:418
  43.4 0.9 %collective-permute-start = (bf16[2,128,128]{2,1,0:T(8,128)(2,1)S(1)}, bf16[2,128,128]{2,1,0:T(8,128)(2,1)S(1)}, u32[]{:S(2)}, u32[]{:S(2)}) collective-permute-start(bf16[2,128,128]{2,1,0:T(8,128)(2,1)S(1)} %collect.3), channel_id=1, source_target_pairs={{0,1},{1,0},{2,3},{3,2},{4,5},{5,4},{6,7},{7,6},{8,9},{9,8},{10,11... | collective-permute-start | bytes 196616 | tf_op jit(solution)/shard_map/ppermute | solution.py:448
  44.3 0.0 copy-done.2
  44.3 0.1 iota_compare_fusion
  44.4 0.8 %collect.2 = f32[2,128,128]{2,1,0:T(8,128)S(1)} custom-call(s32[16,16]{1,0:T(8,128)S(1)} %copy-done, bf16[16,128,128]{2,1,0:T(8,128)(2,1)S(1)} %all_to_all.10.collected_ref), custom_call_target="tpu_custom_call" | custom-call | flops 1000000 | bytes 700000 | tf_op jit(solution)/shard_map/collect/pallas_call | solution.py:418
  45.2 2.5 %collective-permute-done = bf16[2,128,128]{2,1,0:T(8,128)(2,1)S(1)} collective-permute-done((bf16[2,128,128]{2,1,0:T(8,128)(2,1)S(1)}, bf16[2,128,128]{2,1,0:T(8,128)(2,1)S(1)}, u32[]{:S(2)}, u32[]{:S(2)}) %collective-permute-start) | collective-permute-done | bytes 65568 | tf_op jit(solution)/shard_map/ppermute | solution.py:448
  47.7 0.0 copy-done.1
  47.7 0.7 %add_convert_fusion = bf16[2,128,128]{2,1,0:T(8,128)(2,1)} fusion(f32[2,128,128]{2,1,0:T(8,128)S(1)} %collect.2, bf16[2,128,128]{2,1,0:T(8,128)(2,1)S(1)} %collective-permute-done, bf16[2,128,128]{2,1,0:T(8,128)(2,1)S(1)} %copy-done.1, pred[2,128]{1,0:T(4,128)(4,1)S(1)} %iota_compare_fusion), kind=kLoop, calls=%fused_computation | loop fusion | flops 196608 | bytes 327936 | tf_op jit(solution)/shard_map/convert_element_type | solution.py:455
Async XLA Ops:
  1.5 14.9 %all-to-all-start = ((f32[32,4,128]{2,1,0:T(4,128)}), f32[32,4,128]{2,1,0:T(4,128)S(1)}, u32[]{:S(2)}, u32[]{:S(2)}) async-start(f32[32,4,128]{2,1,0:T(4,128)} %offer.1), calls=%async_computation | async-start | bytes 131072 | tf_op jit(solution)/shard_map/all_to_all | solution.py:438
  16.4 26.1 %copy-start = (s32[16,16]{1,0:T(8,128)S(1)}, s32[16,16]{1,0:T(8,128)}, u32[]{:S(2)}) copy-start(s32[16,16]{1,0:T(8,128)} %slot_tile_ref.3) | copy-start | bytes 3076
  24.2 20.1 %copy-start.2 = (s32[2]{0:T(128)S(1)}, s32[2]{0:T(128)}, u32[]{:S(2)}) copy-start(s32[2]{0:T(128)} %test_counts_hbm.1) | copy-start | bytes 28
  24.3 23.4 %copy-start.1 = (bf16[2,128,128]{2,1,0:T(8,128)(2,1)S(1)}, bf16[2,128,128]{2,1,0:T(8,128)(2,1)}, u32[]{:S(2)}) copy-start(bf16[2,128,128]{2,1,0:T(8,128)(2,1)} %param.13) | copy-start | bytes 196612
  43.4 4.3 %collective-permute-start = (bf16[2,128,128]{2,1,0:T(8,128)(2,1)S(1)}, bf16[2,128,128]{2,1,0:T(8,128)(2,1)S(1)}, u32[]{:S(2)}, u32[]{:S(2)}) collective-permute-start(bf16[2,128,128]{2,1,0:T(8,128)(2,1)S(1)} %collect.3), channel_id=1, source_target_pairs={{0,1},{1,0},{2,3},{3,2},{4,5},{5,4},{6,7},{7,6},{8,9},{9,8},{10,11... | collective-permute-start | bytes 196616 | tf_op jit(solution)/shard_map/ppermute | solution.py:448
